TPU v7x, 32 devices: a whole 2x2x4 slice. The times are simulated.
32 devices in a mesh: crop: 2 (over x), ia: 8 (over z, y), ja: 2 (over core).
Axes of the slice: x: 2, y: 2, z: 4, core: 2. Of those that a mesh axis runs over, the one named last changes fastest.
Arguments:
- pair_in: bfloat16 [512, 256, 128], P(('crop', 'ia', 'ja')), parts along dimension 0, may hold values from -6 to 6
- tri_sum: bfloat16 [512, 256, 128], P(('crop', 'ia', 'ja')), parts along dimension 0, may hold values from -6 to 6
- pair_mid: bfloat16 [512, 256, 128], P(('crop', 'ia', 'ja')), parts along dimension 0, may hold values from -6 to 6
- pair_grad: bfloat16 [512, 256, 128], P(('crop', 'ia', 'ja')), parts along dimension 0, may hold values from -6 to 6
- residue_mask: int32 [512], P('crop'), parts along dimension 0, may hold values from 0 to 1, as said below
- tri_gain: float32 [128], replicated, may hold values from 0.1 to 1.9
- w_left: bfloat16 [128, 256], replicated, may hold values from -0.5 to 0.5
- w_right: bfloat16 [128, 256], replicated, may hold values from -0.5 to 0.5
- w_tgate: bfloat16 [128, 128], replicated, may hold values from -0.5 to 0.5
- sum_gain: float32 [128], replicated, may hold values from 0.1 to 1.9
- w_tout: bfloat16 [128, 128], replicated, may hold values from -0.5 to 0.5
- att_gain: float32 [128], replicated, may hold values from 0.1 to 1.9
- w_qkvg: bfloat16 [128, 512], replicated, may hold values from -0.5 to 0.5
- w_bias: bfloat16 [128, 4], replicated, may hold values from -0.5 to 0.5
- w_aout: bfloat16 [128, 128], replicated, may hold values from -0.5 to 0.5
Outputs:
- pair_in_grad: float32 [512, 256, 128], P(('crop', 'ia', 'ja')), parts along dimension 0
There are 2 independent parts, one for each index of `crop`. A program takes and returns all parts, laid end to end along the dimension named above; an argument that names none is the same for every part. Nothing has to cross between parts.
Inputs may be any that keep to these rules, and one draw needn't show every extreme that they name: `residue_mask`: 1 for the first residues of the crop, half of the 256 residues or more, and 0 for the padding that follows them.
All inputs are finite; a program needn't handle non-finite values.
Results may differ from a plain program's by a relative error of at most 0.009.
Values may be sent and summed in bfloat16 or wider, within the bound.
A program may use at most 128 MiB of HBM per device.

v0:
```python
import jax
import jax.numpy as jnp
from jax import lax
from jax.sharding import PartitionSpec as P

EPSILON = 1e-05


def for_sending(array):

    def short(part):
        return part.astype(jnp.bfloat16) if part.dtype == jnp.float32 else part

    return jax.tree.map(short, array)


def from_partner(value, axis, apart):
    mask = 2**apart
    pairs = [(source, source ^ mask) for source in range(lax.axis_size(axis))]
    return lax.ppermute(value, axis, pairs)


def normalize(values_in, gain_row):
    average = jnp.mean(values_in, axis=-1, keepdims=True)
    centred = values_in - average
    second = jnp.mean(centred * centred, axis=-1, keepdims=True)
    return centred * lax.rsqrt(second + EPSILON) * gain_row


def to_planes(values_in, groups):
    band_rows, length, channels = values_in.shape
    return jnp.transpose(values_in, (2, 0, 1)).reshape(
        groups, channels // groups, band_rows, length
    )


def from_planes(values_in, groups, band_rows):
    plane_count = values_in.shape[1]
    length = values_in.shape[3]
    return values_in.reshape(plane_count, groups, band_rows, length)


def to_bands(values_in):
    channels = values_in.shape[0]
    band_rows = values_in.shape[2]
    length = values_in.shape[3]
    return jnp.transpose(values_in.reshape(channels, band_rows, length), (1, 2, 0))


def plane_product(grad_cols, other):
    return jnp.einsum("xcij,xcjk->xcik", grad_cols, other, preferred_element_type=jnp.float32)


def plane_transposed(grad_cols, other):
    return jnp.einsum("xcij,xcik->xcjk", grad_cols, other, preferred_element_type=jnp.float32)


def per_device(
    pair_in,
    tri_sum,
    pair_mid,
    pair_grad,
    residue_mask,
    tri_gain,
    w_left,
    w_right,
    w_tgate,
    sum_gain,
    w_tout,
    att_gain,
    w_qkvg,
    w_bias,
    w_aout,
):
    band_rows, length, channels = pair_in.shape
    head_count = w_bias.shape[1]
    head_dim = channels // head_count
    score_scale = head_dim ** (-0.5)
    key_mask = residue_mask.astype(jnp.float32)
    band_index = lax.axis_index(("ia", "ja"))
    row_mask = lax.dynamic_slice_in_dim(key_mask, band_index * band_rows, band_rows)
    mid_full = pair_mid.astype(jnp.float32)
    normed_mid, mid_pullback = jax.vjp(lambda inside: normalize(inside, att_gain), mid_full)
    mid_flat = normed_mid.astype(jnp.bfloat16).reshape(band_rows * length, channels)
    projected = jnp.dot(mid_flat, w_qkvg, preferred_element_type=jnp.float32).reshape(
        band_rows, length, 4 * channels
    )
    bias_local = jnp.dot(mid_flat, w_bias, preferred_element_type=jnp.float32).astype(jnp.bfloat16)
    bias_local = jnp.transpose(bias_local.reshape(band_rows, length, head_count), (2, 0, 1))
    bias_full = lax.all_gather(bias_local, ("ia", "ja"), axis=1, tiled=True)
    queries_all = projected[..., :channels].astype(jnp.bfloat16)
    keys_all = projected[..., channels : 2 * channels].astype(jnp.bfloat16)
    values_all = projected[..., 2 * channels : 3 * channels].astype(jnp.bfloat16)
    att_gate = jax.nn.sigmoid(projected[..., 3 * channels :])
    gated_grad = jnp.dot(
        pair_grad.reshape(band_rows * length, channels),
        w_aout.T,
        preferred_element_type=jnp.float32,
    ).reshape(band_rows, length, channels)

    def attend_row(running, row_in):
        query_row, key_row, value_row, gate_row, gated_row = row_in
        queries = query_row.reshape(length, head_count, head_dim)
        key_rows = key_row.reshape(length, head_count, head_dim)
        value_rows = value_row.reshape(length, head_count, head_dim)
        scores = (
            jnp.einsum("jhd,khd->hjk", queries, key_rows, preferred_element_type=jnp.float32)
            * score_scale
            + bias_full
        )
        exp_scores = jnp.exp(scores) * key_mask
        probs = exp_scores / jnp.sum(exp_scores, axis=-1, keepdims=True)
        probs_b = probs.astype(jnp.bfloat16)
        attended = jnp.einsum(
            "hjk,khd->jhd", probs_b, value_rows, preferred_element_type=jnp.float32
        ).reshape(length, channels)
        logit_grad = gated_row * attended * gate_row * (1.0 - gate_row)
        out_grad = (gated_row * gate_row).astype(jnp.bfloat16).reshape(length, head_count, head_dim)
        prob_grad = jnp.einsum(
            "jhd,khd->hjk", out_grad, value_rows, preferred_element_type=jnp.float32
        )
        score_grad = probs * (prob_grad - jnp.sum(probs * prob_grad, axis=-1, keepdims=True))
        score_b = score_grad.astype(jnp.bfloat16)
        query_grad = (
            jnp.einsum("hjk,khd->jhd", score_b, key_rows, preferred_element_type=jnp.float32)
            * score_scale
        )
        key_grad = (
            jnp.einsum("hjk,jhd->khd", score_b, queries, preferred_element_type=jnp.float32)
            * score_scale
        )
        value_grad = jnp.einsum(
            "hjk,jhd->khd", probs_b, out_grad, preferred_element_type=jnp.float32
        )
        proj_grad = jnp.concatenate(
            [
                query_grad.reshape(length, channels),
                key_grad.reshape(length, channels),
                value_grad.reshape(length, channels),
                logit_grad,
            ],
            axis=-1,
        ).astype(jnp.bfloat16)
        return (running + score_grad, proj_grad)

    bias_acc, proj_grads = lax.scan(
        attend_row,
        jnp.zeros((head_count, length, length), jnp.float32),
        (queries_all, keys_all, values_all, att_gate, gated_grad),
    )
    bias_band = lax.psum_scatter(bias_acc, ("ia", "ja"), scatter_dimension=1, tiled=True)
    normed_grad = jnp.dot(
        proj_grads.reshape(band_rows * length, 4 * channels),
        w_qkvg.T,
        preferred_element_type=jnp.float32,
    ).reshape(band_rows, length, channels)
    normed_grad = normed_grad + jnp.einsum(
        "hjk,ch->jkc", bias_band, w_bias.astype(jnp.float32), precision=lax.Precision.HIGHEST
    )
    mid_grad = pair_grad.astype(jnp.float32) + mid_pullback(normed_grad)[0]
    in_full = pair_in.astype(jnp.float32)
    normed_in, in_pullback = jax.vjp(lambda inside: normalize(inside, tri_gain), in_full)
    in_flat = normed_in.astype(jnp.bfloat16).reshape(band_rows * length, channels)
    cell_mask = (row_mask[:, None] * key_mask[None, :])[:, :, None]
    left_proj = jnp.dot(in_flat, w_left, preferred_element_type=jnp.float32).reshape(
        band_rows, length, 2 * channels
    )
    left_gate = jax.nn.sigmoid(left_proj[..., :channels])
    left_act = (cell_mask * left_gate * left_proj[..., channels:]).astype(jnp.bfloat16)
    right_proj = jnp.dot(in_flat, w_right, preferred_element_type=jnp.float32).reshape(
        band_rows, length, 2 * channels
    )
    right_gate = jax.nn.sigmoid(right_proj[..., :channels])
    right_act = (cell_mask * right_gate * right_proj[..., channels:]).astype(jnp.bfloat16)
    tri_gate = jax.nn.sigmoid(
        jnp.dot(in_flat, w_tgate, preferred_element_type=jnp.float32)
    ).reshape(band_rows, length, channels)
    sum_normed, sum_pullback = jax.vjp(
        lambda inside: normalize(inside, sum_gain), tri_sum.astype(jnp.float32)
    )
    tri_out = jnp.dot(
        sum_normed.astype(jnp.bfloat16).reshape(band_rows * length, channels),
        w_tout,
        preferred_element_type=jnp.float32,
    ).reshape(band_rows, length, channels)
    tout_grad = (mid_grad * tri_gate).astype(jnp.bfloat16).reshape(band_rows * length, channels)
    gate_back = (
        (mid_grad * tri_out * tri_gate * (1.0 - tri_gate))
        .astype(jnp.bfloat16)
        .reshape(band_rows * length, channels)
    )
    summed_grad = jnp.dot(tout_grad, w_tout.T, preferred_element_type=jnp.float32).reshape(
        band_rows, length, channels
    )
    sum_grad = sum_pullback(summed_grad)[0].astype(jnp.bfloat16)
    groups = lax.axis_size("ia")
    parity = lax.axis_index("ja")
    stacked = (
        to_planes(sum_grad, groups),
        to_planes(left_act, groups),
        to_planes(right_act, groups),
    )
    pieces = (
        lax.all_to_all(stacked[0], "ia", split_axis=0, concat_axis=2, tiled=True),
        lax.all_to_all(stacked[1], "ia", split_axis=0, concat_axis=2, tiled=True),
        lax.all_to_all(stacked[2], "ia", split_axis=0, concat_axis=2, tiled=True),
    )
    partner = jax.tree.map(
        lambda part, own: part.astype(own.dtype), from_partner(for_sending(pieces), "ja", 0), pieces
    )
    grad_own, left_own, right_own = pieces
    grad_other, left_other, right_other = partner
    plane_count = grad_own.shape[1]
    local_rows = grad_own.shape[2]

    def columns(grad_plane, chosen):
        reshaped = grad_plane.reshape(1, plane_count, local_rows, groups, 2, band_rows)
        picked = lax.dynamic_index_in_dim(reshaped, chosen, 4, keepdims=False)
        return picked.reshape(1, plane_count, local_rows, local_rows)

    own_cols = columns(grad_own, parity)
    far_cols = columns(grad_own, 1 - parity)
    other_cols = columns(grad_other, parity)
    left_out = (plane_product(own_cols, right_own) + plane_product(far_cols, right_other)).astype(
        jnp.bfloat16
    )
    right_out = (
        plane_transposed(own_cols, left_own) + plane_transposed(other_cols, left_other)
    ).astype(jnp.bfloat16)
    left_back_planes, right_back_planes = (
        lax.all_to_all(
            from_planes(left_out, groups, band_rows), "ia", split_axis=1, concat_axis=0, tiled=True
        ),
        lax.all_to_all(
            from_planes(right_out, groups, band_rows), "ia", split_axis=1, concat_axis=0, tiled=True
        ),
    )
    left_grad = to_bands(left_back_planes).astype(jnp.float32)
    right_grad = to_bands(right_back_planes).astype(jnp.float32)
    left_back = (
        jnp.concatenate(
            [
                left_grad * cell_mask * left_proj[..., channels:] * left_gate * (1.0 - left_gate),
                left_grad * cell_mask * left_gate,
            ],
            axis=-1,
        )
        .astype(jnp.bfloat16)
        .reshape(band_rows * length, 2 * channels)
    )
    right_back = (
        jnp.concatenate(
            [
                right_grad
                * cell_mask
                * right_proj[..., channels:]
                * right_gate
                * (1.0 - right_gate),
                right_grad * cell_mask * right_gate,
            ],
            axis=-1,
        )
        .astype(jnp.bfloat16)
        .reshape(band_rows * length, 2 * channels)
    )
    normed_in_grad = jnp.dot(left_back, w_left.T, preferred_element_type=jnp.float32)
    normed_in_grad = normed_in_grad + jnp.dot(
        right_back, w_right.T, preferred_element_type=jnp.float32
    )
    normed_in_grad = normed_in_grad + jnp.dot(
        gate_back, w_tgate.T, preferred_element_type=jnp.float32
    )
    return mid_grad + in_pullback(normed_in_grad.reshape(band_rows, length, channels))[0]


def solution(mesh):
    placed = (
        P(("crop", "ia", "ja"), None, None),
        P(("crop", "ia", "ja"), None, None),
        P(("crop", "ia", "ja"), None, None),
        P(("crop", "ia", "ja"), None, None),
        P("crop"),
        P(),
        P(),
        P(),
        P(),
        P(),
        P(),
        P(),
        P(),
        P(),
        P(),
    )
    return jax.shard_map(
        per_device,
        mesh=mesh,
        in_specs=placed,
        out_specs=P(("crop", "ia", "ja"), None, None),
        check_vma=False,
    )
```

profile of v0, /device:TPU:0, one launch (start us, length us, event | category | flops | bytes accessed | tf_op | source)
XLA Modules:
  0.0 710.5 jit_solution(15861655189240374120)
XLA Ops:
  17.6 24.6 %all_gather.3 = bf16[4,256,256]{2,0,1:T(4,128)(2,1)S(1)} all-gather(bf16[4,16,256]{2,0,1:T(4,128)(2,1)S(1)} %bitcast.252), channel_id=1, replica_groups=mesh['crop'=2,'ia'=8,'ja'=2] {'ia','ja'}, dimensions={1}, use_global_device_ids=true | all-gather | bytes 557056 | tf_op jit(solution)/shard_map/all_gather | solution.py:90
  43.9 3.0 fusion.91
  46.9 290.3 %while.13 = (s32[]{:T(128)}, f32[4,256,256]{1,2,0:T(8,128)S(1)}, bf16[16,256,512]{1,2,0:T(8,128)(2,1)}, bf16[16,256,128]{2,1,0:T(8,128)(2,1)}, bf16[16,256,128]{...) while((s32[]{:T(128)}, f32[4,256,256]{1,2,0:T(8,128)S(1)}, ...), condition=%wide.region_5.6_spmd.clone, body=%wide.region_2.5_spmd.clone.sunk | while | flops 124128000 | bytes 21703452 | solution.py:146
  57.4 2.6 multiply_reduce_fusion.2
  148.1 2.6 multiply_reduce_fusion.2
  184.4 2.6 multiply_reduce_fusion.2
  220.7 2.6 multiply_reduce_fusion.2
  348.9 4.4 all-to-all-start.3
  356.4 3.4 fusion.19
  359.8 2.6 fusion.80
  362.4 76.3 %all-reduce.3.cloned.1.call-done = f32[4,256,256]{2,0,1:T(4,128)} async-done(((f32[4,256,256]{2,0,1:T(4,128)}), f32[4,256,256]{2,0,1:T(4,128)}) %all-reduce.3.cloned.1.call-update) | async-done | bytes 1048592
  438.8 4.6 fusion.35
  453.0 3.9 all-to-all-start
  459.2 22.7 %all-to-all-done = bf16[8,16,16,256]{3,2,1,0:T(8,128)(2,1)S(1)} async-done(((bf16[8,16,16,256]{3,2,1,0:T(8,128)(2,1)}), bf16[8,16,16,256]{3,2,1,0:T(8,128)(2,1)S(1)}, u32[]{:S(2)}, u32[]{:S(2)}) %all-to-all-start) | async-done | bytes 1048608 | tf_op jit(solution)/shard_map/all_to_all | solution.py:204
  483.1 25.8 %reshape.353 = bf16[1,16,128,8,2,16]{5,4,3,2,1,0:T(2,128)(2,1)} reshape(bf16[1,16,8,16,256]{4,3,2,1,0:T(8,128)(2,1)} %bitcast.130.clone.2) | data formatting | bytes 2097152 | tf_op jit(solution)/shard_map/reshape | solution.py:217
  508.8 20.5 %constant_dynamic-slice_fusion.5 = (bf16[1,16,128,8,1,16]{5,4,3,2,1,0:T(2,128)(2,1)}, bf16[1,16,128,8,1,16]{5,4,3,2,1,0:T(2,128)(2,1)}) fusion(bf16[1,16,128,8,2,16]{5,4,3,2,1,0:T(2,128)(2,1)} %reshape.353, s32[]{:T(128)S(6)} %select_n.13, s32[]{:T(128)S(6)} %select_n.11), kind=kLoop, calls=%fused_computation.156 | loop fusion | bytes 2097160 | tf_op jit(solution)/shard_map/jit(dynamic_index_in_dim)/dynamic_slice | solution.py:218
  529.4 17.4 %copy.111 = bf16[1,16,128,8,1,16]{2,5,4,3,1,0:T(8,128)(2,1)S(1)} copy(bf16[1,16,128,8,1,16]{5,4,3,2,1,0:T(2,128)(2,1)} %get-tuple-element.154) | data formatting | bytes 1048576
  546.8 3.2 fusion.105
  556.7 4.2 all-to-all-start.4
  561.0 2.7 fusion.87
  563.7 24.0 %all-to-all-done.4 = bf16[16,8,16,256]{3,2,0,1:T(8,128)(2,1)} async-done(((bf16[16,8,16,256]{3,2,0,1:T(8,128)(2,1)}), bf16[16,8,16,256]{3,2,0,1:T(8,128)(2,1)}, u32[]{:S(2)}, u32[]{:S(2)}) %all-to-all-start.4) | async-done | bytes 1048608 | tf_op jit(solution)/shard_map/all_to_all | solution.py:234
  587.7 2.8 bitcast_convert_fusion
  590.5 2.9 copy.95
  593.5 5.5 fusion.62
  600.6 29.6 %all_to_all.72 = bf16[8,16,16,256]{3,2,1,0:T(8,128)(2,1)S(1)} all-to-all(bf16[8,16,16,256]{3,2,1,0:T(8,128)(2,1)} %bitcast.242), channel_id=1, replica_groups=mesh['crop'=2,'ia'=8,'ja'=2] {'ia'}, dimensions={0} | all-to-all | bytes 2097152 | tf_op jit(solution)/shard_map/all_to_all | solution.py:206
  631.3 18.9 %copy.112 = bf16[1,16,128,8,1,16]{2,5,4,3,1,0:T(8,128)(2,1)} copy(bf16[1,16,128,8,1,16]{5,4,3,2,1,0:T(2,128)(2,1)} %get-tuple-element.153) | data formatting | bytes 1048576
  654.9 3.8 all-to-all-start.2
  658.7 4.0 multiply_convert_fusion.1
  662.7 22.4 %all-to-all-done.2 = bf16[16,8,16,256]{3,2,0,1:T(8,128)(2,1)S(1)} async-done(((bf16[16,8,16,256]{3,2,0,1:T(8,128)(2,1)}), bf16[16,8,16,256]{3,2,0,1:T(8,128)(2,1)S(1)}, u32[]{:S(2)}, u32[]{:S(2)}) %all-to-all-start.2) | async-done | bytes 1048608 | tf_op jit(solution)/shard_map/all_to_all | solution.py:231
  686.7 3.0 copy.89
  689.7 3.3 fusion.66
  700.2 3.5 add_add_fusion.3
  (564 shorter events, 340.4 us)
Async XLA Ops:
  6.5 5.4 copy-start
  6.5 4.1 copy-start.2
  6.5 4.1 copy-start.36
  6.5 432.2 %all-reduce.3.cloned.1.call-start = ((), (), s32[]{:S(2)}) async-start(), calls=%async_computation.5 | async-start | bytes 2097152
  17.3 26.1 %copy-start.38 = (s32[256]{0:T(256)S(1)}, s32[256]{0:T(256)}, u32[]{:S(2)}) copy-start(s32[256]{0:T(256)} %param.21) | copy-start | bytes 3076
  17.3 26.6 %copy-start.30 = (bf16[128,128]{1,0:T(8,128)(2,1)S(1)}, bf16[128,128]{1,0:T(8,128)(2,1)}, u32[]{:S(2)}) copy-start(bf16[128,128]{1,0:T(8,128)(2,1)} %param.31) | copy-start | bytes 98308
  50.3 2.7 copy-start.7
  86.6 2.7 copy-start.7
  122.8 2.7 copy-start.7
  195.4 2.7 copy-start.7
  231.7 2.7 copy-start.7
  249.9 2.7 copy-start.7
  338.5 3.1 copy-start.33
  338.5 5.3 copy-start.25
  348.9 104.1 %all-to-all-start.3 = ((bf16[8,16,16,256]{3,2,1,0:T(8,128)(2,1)}), bf16[8,16,16,256]{3,2,1,0:T(8,128)(2,1)}, u32[]{:S(2)}, u32[]{:S(2)}) async-start(bf16[8,16,16,256]{3,2,1,0:T(8,128)(2,1)} %bitcast.241), calls=%async_computation.3 | async-start | bytes 2097152 | tf_op jit(solution)/shard_map/all_to_all | solution.py:205
  353.4 2.9 copy-start.31
  356.3 3.5 copy-start.21
  359.8 78.9 %copy-start.35 = (bf16[128,4]{0,1:T(4,128)(2,1)S(1)}, bf16[128,4]{0,1:T(4,128)(2,1)}, u32[]{:S(2)}) copy-start(bf16[128,4]{0,1:T(4,128)(2,1)} %param.30) | copy-start | bytes 3076
  359.8 78.9 %copy-start.37 = (f32[128]{0:T(128)S(1)}, f32[128]{0:T(128)}, u32[]{:S(2)}) copy-start(f32[128]{0:T(128)} %param.28) | copy-start | bytes 1540
  362.4 80.9 %copy-start.28 = (f32[16,256]{1,0:T(8,128)S(1)}, f32[16,256]{1,0:T(8,128)}, u32[]{:S(2)}) copy-start(f32[16,256]{1,0:T(8,128)} %copy-done.27) | copy-start | bytes 49156
  362.4 81.0 %copy-start.24 = (f32[16,256]{1,0:T(8,128)S(1)}, f32[16,256]{1,0:T(8,128)}, u32[]{:S(2)}) copy-start(f32[16,256]{1,0:T(8,128)} %copy-done.23) | copy-start | bytes 49156
  453.0 28.9 %all-to-all-start = ((bf16[8,16,16,256]{3,2,1,0:T(8,128)(2,1)}), bf16[8,16,16,256]{3,2,1,0:T(8,128)(2,1)S(1)}, u32[]{:S(2)}, u32[]{:S(2)}) async-start(bf16[8,16,16,256]{3,2,1,0:T(8,128)(2,1)} %copy.80), calls=%async_computation | async-start | bytes 2097152 | tf_op jit(solution)/shard_map/all_to_all | solution.py:204
  459.2 94.1 %collective-permute-start.2 = (bf16[1,16,128,256]{3,2,1,0:T(8,128)(2,1)}, bf16[1,16,128,256]{3,2,1,0:T(8,128)(2,1)}, u32[]{:S(2)}, u32[]{:S(2)}) collective-permute-start(bf16[1,16,128,256]{3,2,1,0:T(8,128)(2,1)} %bitcast.42), channel_id=1, source_target_pairs={{0,1},{1,0},{2,3},{3,2},{4,5},{5,4},{6,7},{7,6},{8,9},{9,8},{10,11... | collective-permute-start | bytes 3145736 | tf_op jit(solution)/shard_map/ppermute | solution.py:20
  508.8 41.1 %collective-permute-start.1 = (bf16[1,16,128,256]{3,2,1,0:T(8,128)(2,1)}, bf16[1,16,128,256]{3,2,1,0:T(8,128)(2,1)}, u32[]{:S(2)}, u32[]{:S(2)}) collective-permute-start(bf16[1,16,128,256]{3,2,1,0:T(8,128)(2,1)} %bitcast.38), channel_id=1, source_target_pairs={{0,1},{1,0},{2,3},{3,2},{4,5},{5,4},{6,7},{7,6},{8,9},{9,8},{10,11... | collective-permute-start | bytes 3145736 | tf_op jit(solution)/shard_map/ppermute | solution.py:20
  546.8 5.5 copy-start.15
  555.7 5.3 copy-start.9
  555.7 5.3 copy-start.26
  556.7 31.0 %all-to-all-start.4 = ((bf16[16,8,16,256]{3,2,0,1:T(8,128)(2,1)}), bf16[16,8,16,256]{3,2,0,1:T(8,128)(2,1)}, u32[]{:S(2)}, u32[]{:S(2)}) async-start(bf16[16,8,16,256]{3,2,0,1:T(8,128)(2,1)} %copy.94), calls=%async_computation.4 | async-start | bytes 2097152 | tf_op jit(solution)/shard_map/all_to_all | solution.py:234
  631.3 20.7 %collective-permute-start = (bf16[1,16,128,256]{3,2,1,0:T(8,128)(2,1)}, bf16[1,16,128,256]{3,2,1,0:T(8,128)(2,1)}, u32[]{:S(2)}, u32[]{:S(2)}) collective-permute-start(bf16[1,16,128,256]{3,2,1,0:T(8,128)(2,1)} %bitcast.23), channel_id=1, source_target_pairs={{0,1},{1,0},{2,3},{3,2},{4,5},{5,4},{6,7},{7,6},{8,9},{9,8},{10,11... | collective-permute-start | bytes 3145736 | tf_op jit(solution)/shard_map/ppermute | solution.py:20
  631.3 18.9 %copy-start.16 = (bf16[1,16,128,8,1,16]{2,5,4,3,1,0:T(8,128)(2,1)S(1)}, bf16[1,16,128,8,1,16]{2,5,4,3,1,0:T(8,128)(2,1)}, u32[]{:S(2)}) copy-start(bf16[1,16,128,8,1,16]{2,5,4,3,1,0:T(8,128)(2,1)} %copy-done.15) | copy-start | bytes 1572868
  654.9 30.2 %all-to-all-start.2 = ((bf16[16,8,16,256]{3,2,0,1:T(8,128)(2,1)}), bf16[16,8,16,256]{3,2,0,1:T(8,128)(2,1)S(1)}, u32[]{:S(2)}, u32[]{:S(2)}) async-start(bf16[16,8,16,256]{3,2,0,1:T(8,128)(2,1)} %copy.88), calls=%async_computation.2 | async-start | bytes 2097152 | tf_op jit(solution)/shard_map/all_to_all | solution.py:231
  700.1 3.5 copy-start.1
  (91 other events, 153.1 us)
Sparse Core Ops, SparseCore 0:
  338.6 100.0 all-reduce.2
where the time goes:
time: 717 us; the launch traced here: 710 us
  local copies, waits for them, and re-layouts  200 us (28%)
  matrix products  171 us (24%)
  waiting for transfers between devices  146 us (20%)
  other arithmetic  107 us (15%)
  blocking collectives  54.1 us (8%)
  starting transfers between devices  16.4 us (2%)
  between operations  14.7 us (2%)
    unnamed x2, waiting for transfers between devices  76.3 us
    dynamic_slice x112, local copies, waits for them, and re-layouts, per_device(): lax.scan(attend_row, jnp.zeros((head_count, length, length), jnp.float32)...  74.2 us
    unnamed x75, local copies, waits for them, and re-layouts  44.3 us
    div x16, matrix products, attend_row(): probs = exp_scores / jnp.sum(exp_scores, axis=-1, keepdims=True)  41.8 us
    another operation x18, other arithmetic  34.8 us
    dot_general x16, matrix products, attend_row(): jnp.einsum('hjk,jhd->khd', probs_b, out_grad, preferred_element_type=jnp....  30.1 us
    convert_element_type x16, other arithmetic, attend_row(): score_b = score_grad.astype(jnp.bfloat16)  29.8 us
    all_to_all x1, blocking collectives, per_device(): lax.all_to_all(stacked[2], 'ia', split_axis=0, concat_axis=2, tiled=True)  29.6 us
  transfers between devices with their start and end apart: 8, of which 4 were waited for; matrix products, arithmetic and copies ran while one was open for 18% of the time, Pallas kernels for 0%

commit v1 on v0

v1 whole, which is shorter than its diff:
```python
import functools
import math

import jax
import jax.numpy as jnp
from jax import lax
from jax.experimental import pallas as pl
from jax.experimental.pallas import tpu as pltpu
from jax.sharding import PartitionSpec as P

EPSILON = 1e-05
F32 = jnp.float32
BF16 = jnp.bfloat16
VMEM_BYTES = 48 * 1024 * 1024
AXES = ("ia", "ja")


def dot(a, b):
    return jnp.dot(a, b, preferred_element_type=F32)


def dot_t(a, b):
    return lax.dot_general(a, b, (((1,), (1,)), ((), ())), preferred_element_type=F32)


def standardize(v):
    average = jnp.mean(v, axis=-1, keepdims=True)
    centred = v - average
    second = jnp.mean(centred * centred, axis=-1, keepdims=True)
    rstd = lax.rsqrt(second + EPSILON)
    return centred * rstd, rstd


def norm_grad(unit, rstd, gain, cotangent):
    g = cotangent * gain
    return rstd * (
        g
        - jnp.mean(g, axis=-1, keepdims=True)
        - unit * jnp.mean(g * unit, axis=-1, keepdims=True)
    )


def rows_of(ref):
    block = ref[...]
    return block.reshape(block.shape[0] * block.shape[1], block.shape[2])


def put_planes(ref, r, value, split):
    if split:
        ref[:, r] = value.reshape(ref.shape[0], ref.shape[2], ref.shape[3]).astype(BF16)
    else:
        ref[r] = value.astype(BF16)


def get_planes(ref, r, split):
    if split:
        value = ref[:, r].astype(F32)
        return value.reshape(value.shape[0] * value.shape[1], value.shape[2])
    return ref[r].astype(F32)


def edge_kernel(split, pin_ref, cell_ref, gain_ref, wt_ref, left_ref, right_ref):
    block, length, channels = pin_ref.shape
    unit, _ = standardize(rows_of(pin_ref).astype(F32))
    normed = (unit * gain_ref[...]).astype(BF16)
    proj = dot_t(wt_ref[...], normed)
    for r in range(block):
        part = proj[:, r * length : (r + 1) * length]
        cell = cell_ref[r]
        left = cell * jax.nn.sigmoid(part[:channels]) * part[channels : 2 * channels]
        right = (
            cell * jax.nn.sigmoid(part[2 * channels : 3 * channels]) * part[3 * channels :]
        )
        put_planes(left_ref, r, left, split)
        put_planes(right_ref, r, right, split)


def attention_kernel(
    heads,
    mid_ref,
    grad_ref,
    gain_ref,
    wt_ref,
    wkv_ref,
    wqg_ref,
    wtkv_ref,
    waout_ref,
    bias_ref,
    out_ref,
    bias_out_ref,
    q_block,
    o_block,
    acc,
):
    step = pl.program_id(0)
    length, channels = mid_ref.shape[1:]
    dim = channels // heads
    scale = dim ** (-0.5)

    @pl.when(step == 0)
    def _():
        q_block[...] = jnp.zeros_like(q_block)
        o_block[...] = jnp.zeros_like(o_block)
        acc[...] = jnp.zeros_like(acc)

    unit, _ = standardize(mid_ref[0].astype(F32))
    normed = (unit * gain_ref[...]).astype(BF16)
    proj = dot_t(wt_ref[...], normed)
    kv = dot(normed, wkv_ref[...]).astype(BF16)
    keys, values = kv[:, :channels], kv[:, channels:]
    keys_t = proj[channels : 2 * channels].astype(BF16)
    values_t = proj[2 * channels : 3 * channels].astype(BF16)
    queries_t = proj[:channels].astype(BF16)
    gate = jax.nn.sigmoid(proj[3 * channels :])
    gated = dot_t(waout_ref[...], grad_ref[0])
    out_t = (gated * gate).astype(BF16)
    for h in range(heads):
        rows = slice(h * dim, (h + 1) * dim)
        q_block[h, rows] = queries_t[rows]
        o_block[h, rows] = out_t[rows]
    attended, query_grads = [], []
    key_grad = jnp.zeros((length, channels), F32)
    value_grad = jnp.zeros((length, channels), F32)
    for h in range(heads):
        rows = slice(h * dim, (h + 1) * dim)
        scores = dot(keys, q_block[h])
        e = jnp.exp2(scores * (scale * math.log2(math.e)) + bias_ref[h])
        probs = e * (1.0 / jnp.sum(e, axis=0, keepdims=True))
        probs_b = probs.astype(BF16)
        prob_grad = dot(values, o_block[h])
        weighted = probs * prob_grad
        score_grad = weighted - probs * jnp.sum(weighted, axis=0, keepdims=True)
        score_b = score_grad.astype(BF16)
        acc[h] += score_grad
        attended.append(dot(values_t[rows], probs_b))
        query_grads.append(dot(keys_t[rows], score_b))
        key_grad += dot_t(score_b, q_block[h])
        value_grad += dot_t(probs_b, o_block[h])
    attended = jnp.concatenate(attended, axis=0)
    query_grad = jnp.concatenate(query_grads, axis=0) * scale
    logit_grad = gated * attended * gate * (1.0 - gate)
    qg = jnp.concatenate([query_grad, logit_grad], axis=0).astype(BF16)
    kv_grad = jnp.concatenate([key_grad * scale, value_grad], axis=1).astype(BF16)
    out_ref[0] = dot(kv_grad, wtkv_ref[...]) + dot(wqg_ref[...], qg).T

    @pl.when(step == pl.num_programs(0) - 1)
    def _():
        for h in range(heads):
            bias_out_ref[h] = acc[h].T.astype(BF16)


def middle_kernel(
    split,
    heads,
    ng_ref,
    band_ref,
    wb_ref,
    mid_ref,
    grad_ref,
    pin_ref,
    sum_ref,
    att_gain_ref,
    tri_gain_ref,
    sum_gain_ref,
    wtgate_ref,
    wtout_ref,
    wtout_t_ref,
    mid_out_ref,
    back_ref,
    planes_ref,
):
    block, length, channels = mid_ref.shape
    bias = []
    for r in range(block):
        band = band_ref[r].T
        part = band[:, 0:1] * wb_ref[0:1]
        for h in range(1, heads):
            part = part + band[:, h : h + 1] * wb_ref[h : h + 1]
        bias.append(part)
    bias = jnp.concatenate(bias, axis=0)
    unit, rstd = standardize(rows_of(mid_ref).astype(F32))
    mid_grad = rows_of(grad_ref).astype(F32) + norm_grad(
        unit, rstd, att_gain_ref[...], rows_of(ng_ref) + bias
    )
    unit, _ = standardize(rows_of(pin_ref).astype(F32))
    gate = jax.nn.sigmoid(dot((unit * tri_gain_ref[...]).astype(BF16), wtgate_ref[...]))
    unit, rstd = standardize(rows_of(sum_ref).astype(F32))
    tri_out = dot((unit * sum_gain_ref[...]).astype(BF16), wtout_ref[...])
    gated = mid_grad * gate
    summed = dot(gated.astype(BF16), wtout_t_ref[...])
    back = gated * tri_out * (1.0 - gate)
    mid_out_ref[...] = mid_grad.reshape(block, length, channels)
    back_ref[...] = back.astype(BF16).reshape(block, length, channels)
    sum_grad = norm_grad(unit, rstd, sum_gain_ref[...], summed)
    for r in range(block):
        put_planes(planes_ref, r, sum_grad[r * length : (r + 1) * length].T, split)


def left_kernel(grad_ref, right_ref, out_ref):
    planes = grad_ref.shape[0]
    outs = []
    for c in range(planes):
        outs.append(dot(grad_ref[c], right_ref[c]))
    if planes % 8 == 0:
        out_ref[...] = jnp.swapaxes(jnp.stack(outs, axis=0), 0, 1).astype(BF16)
    else:
        for c in range(planes):
            out_ref[c] = outs[c].astype(BF16)


def right_kernel(grad_ref, left_ref, out_ref):
    planes = grad_ref.shape[0]
    outs = []
    for c in range(planes):
        outs.append(dot(grad_ref[c].T, left_ref[c]))
    if planes % 8 == 0:
        out_ref[...] = jnp.swapaxes(jnp.stack(outs, axis=0), 0, 1).astype(BF16)
    else:
        for c in range(planes):
            out_ref[c] = outs[c].astype(BF16)


def final_kernel(
    split,
    left_ref,
    right_ref,
    back_ref,
    mid_ref,
    pin_ref,
    cell_ref,
    gain_ref,
    wt_ref,
    wleft_ref,
    wright_ref,
    wtgate_t_ref,
    out_ref,
):
    block, length, channels = pin_ref.shape
    unit, rstd = standardize(rows_of(pin_ref).astype(F32))
    normed = (unit * gain_ref[...]).astype(BF16)
    proj = dot_t(wt_ref[...], normed)

    def backward(grad, part):
        s = jax.nn.sigmoid(part[:channels])
        gs = grad * s
        return jnp.concatenate([gs * part[channels:] * (1.0 - s), gs], axis=0).astype(BF16)

    grads = []
    for r in range(block):
        part = proj[:, r * length : (r + 1) * length]
        cell = cell_ref[r]
        left = backward(get_planes(left_ref, r, split) * cell, part[: 2 * channels])
        right = backward(get_planes(right_ref, r, split) * cell, part[2 * channels :])
        grads.append((dot(wleft_ref[...], left) + dot(wright_ref[...], right)).T)
    total = jnp.concatenate(grads, axis=0) + dot(rows_of(back_ref), wtgate_t_ref[...])
    result = rows_of(mid_ref) + norm_grad(unit, rstd, gain_ref[...], total)
    out_ref[...] = result.reshape(block, length, channels)


def whole(array):
    zeros = (0,) * array.ndim
    return pl.BlockSpec(array.shape, lambda i: zeros)


def banded(array, block):
    rest = array.shape[1:]
    zeros = (0,) * len(rest)
    return pl.BlockSpec((block,) + rest, lambda i: (i,) + zeros)


def params():
    return pltpu.CompilerParams(
        dimension_semantics=("arbitrary",), vmem_limit_bytes=VMEM_BYTES
    )


def per_device(
    pair_in,
    tri_sum,
    pair_mid,
    pair_grad,
    residue_mask,
    tri_gain,
    w_left,
    w_right,
    w_tgate,
    sum_gain,
    w_tout,
    att_gain,
    w_qkvg,
    w_bias,
    w_aout,
):
    rows, length, channels = pair_in.shape
    heads = w_bias.shape[1]
    devices = length // rows
    group = channels // devices
    split = group % 8 == 0
    block = math.gcd(rows, 4)
    key_mask = residue_mask.astype(F32)
    band_index = lax.axis_index(AXES)
    row_mask = lax.dynamic_slice_in_dim(key_mask, band_index * rows, rows)
    cell = (row_mask[:, None] * key_mask[None, :])[:, None, :]
    tri_gain, sum_gain, att_gain = tri_gain[None], sum_gain[None], att_gain[None]
    wt_edges = jnp.concatenate([w_left.T, w_right.T], axis=0)
    wt_qkvg = w_qkvg.T
    w_kv = w_qkvg[:, channels : 3 * channels]
    w_qg = jnp.concatenate([w_qkvg[:, :channels], w_qkvg[:, 3 * channels :]], axis=1)
    wt_kv = wt_qkvg[channels : 3 * channels]

    unit, _ = standardize(pair_mid.astype(F32))
    normed_mid = (unit * att_gain).astype(BF16)
    bias_local = lax.dot_general(
        w_bias, normed_mid, (((0,), (2,)), ((), ())), preferred_element_type=F32
    ).astype(BF16)
    bias_full = lax.all_gather(bias_local, AXES, axis=1, tiled=True)
    bias_t = jnp.swapaxes(bias_full, 1, 2).astype(F32) * math.log2(math.e)
    bias_t = bias_t + jnp.where(residue_mask > 0, 0.0, -1e30)[None, :, None]

    if split:
        plane_shape = jax.ShapeDtypeStruct((devices, rows, group, length), BF16)
        plane_spec = pl.BlockSpec((devices, block, group, length), lambda i: (0, i, 0, 0))
    else:
        plane_shape = jax.ShapeDtypeStruct((rows, channels, length), BF16)
        plane_spec = pl.BlockSpec((block, channels, length), lambda i: (i, 0, 0))

    def spread(planes):
        if not split:
            planes = jnp.swapaxes(planes.reshape(rows, devices, group, length), 0, 1)
        gathered = lax.all_to_all(planes, AXES, split_axis=0, concat_axis=0, tiled=True)
        return jnp.swapaxes(gathered.reshape(length, group, length), 0, 1)

    def collect(planes):
        if not split:
            planes = jnp.swapaxes(planes, 0, 1)
        planes = planes.reshape(devices, rows, group, length)
        back = lax.all_to_all(planes, AXES, split_axis=0, concat_axis=0, tiled=True)
        if not split:
            back = jnp.swapaxes(back, 0, 1).reshape(rows, channels, length)
        return back

    def run(kernel, args, banded_count, out_shape, out_specs, special=()):
        specs = [banded(a, block) for a in args[:banded_count]]
        specs += [whole(a) for a in args[banded_count:]]
        for position, spec in special:
            specs[position] = spec
        return pl.pallas_call(
            kernel,
            grid=(rows // block,),
            in_specs=specs,
            out_specs=out_specs,
            out_shape=out_shape,
            compiler_params=params(),
        )(*args)

    left_act, right_act = run(
        functools.partial(edge_kernel, split),
        (pair_in, cell, tri_gain, wt_edges),
        2,
        (plane_shape, plane_shape),
        (plane_spec, plane_spec),
    )
    left_planes, right_planes = spread(left_act), spread(right_act)

    attention_args = (
        pair_mid,
        pair_grad,
        att_gain,
        wt_qkvg,
        w_kv,
        w_qg,
        wt_kv,
        w_aout,
        bias_t,
    )
    normed_grad, bias_part = pl.pallas_call(
        functools.partial(attention_kernel, heads),
        grid=(rows,),
        in_specs=[banded(a, 1) for a in attention_args[:2]]
        + [whole(a) for a in attention_args[2:]],
        out_specs=(
            pl.BlockSpec((1, length, channels), lambda i: (i, 0, 0)),
            pl.BlockSpec((heads, length, length), lambda i: (0, 0, 0)),
        ),
        out_shape=(
            jax.ShapeDtypeStruct((rows, length, channels), F32),
            jax.ShapeDtypeStruct((heads, length, length), BF16),
        ),
        scratch_shapes=[
            pltpu.VMEM((heads, channels, length), BF16),
            pltpu.VMEM((heads, channels, length), BF16),
            pltpu.VMEM((heads, length, length), F32),
        ],
        compiler_params=params(),
        cost_estimate=pl.CostEstimate(
            flops=rows * heads * 12 * length * length * channels,
            bytes_accessed=rows * length * channels * 8,
            transcendentals=rows * heads * length * length,
        ),
    )(*attention_args)
    bias_part = jnp.swapaxes(bias_part.reshape(heads, devices, rows, length), 0, 1)
    bias_parts = lax.all_to_all(bias_part, AXES, split_axis=0, concat_axis=0, tiled=True)
    band = jnp.swapaxes(jnp.sum(bias_parts.astype(F32), axis=0), 0, 1)
    band = jnp.pad(band, ((0, 0), (0, -heads % 8), (0, 0)))

    row_spec = pl.BlockSpec((block, length, channels), lambda i: (i, 0, 0))
    row_shape = jax.ShapeDtypeStruct((rows, length, channels), F32)
    wb_t = jnp.pad(w_bias.astype(F32).T, ((0, -heads % 8), (0, 0)))
    mid_grad, gate_back, sum_grad = pl.pallas_call(
        functools.partial(middle_kernel, split, heads),
        grid=(rows // block,),
        in_specs=[banded(normed_grad, block), banded(band, block), whole(wb_t)]
        + [row_spec] * 4
        + [whole(a) for a in (att_gain, tri_gain, sum_gain, w_tgate, w_tout, w_tout)],
        out_specs=(row_spec, row_spec, plane_spec),
        out_shape=(row_shape, jax.ShapeDtypeStruct(row_shape.shape, BF16), plane_shape),
        compiler_params=params(),
    )(
        normed_grad,
        band,
        wb_t,
        pair_mid,
        pair_grad,
        pair_in,
        tri_sum,
        att_gain,
        tri_gain,
        sum_gain,
        w_tgate,
        w_tout,
        w_tout.T,
    )
    grad_planes = spread(sum_grad)

    def product(kernel, other):
        shape = (length, group, length) if split else (group, length, length)
        return pl.pallas_call(
            kernel,
            in_specs=[pl.BlockSpec(memory_space=pltpu.VMEM)] * 2,
            out_specs=pl.BlockSpec(memory_space=pltpu.VMEM),
            out_shape=jax.ShapeDtypeStruct(shape, BF16),
            compiler_params=pltpu.CompilerParams(vmem_limit_bytes=VMEM_BYTES),
        )(grad_planes, other)

    left_grad = collect(product(left_kernel, right_planes))
    right_grad = collect(product(right_kernel, left_planes))
    return run(
        functools.partial(final_kernel, split),
        (
            left_grad,
            right_grad,
            gate_back,
            mid_grad,
            pair_in,
            cell,
            tri_gain,
            wt_edges,
            w_left,
            w_right,
            w_tgate.T,
        ),
        6,
        row_shape,
        row_spec,
        special=((0, plane_spec), (1, plane_spec)),
    )


def solution(mesh):
    rows = P(("crop", "ia", "ja"), None, None)
    placed = (rows, rows, rows, rows, P("crop")) + (P(),) * 10
    return jax.shard_map(
        per_device, mesh=mesh, in_specs=placed, out_specs=rows, check_vma=False
    )
```

time: 717 us -> 251 us (0.35)
  local copies, waits for them, and re-layouts: 200 us -> 17.2 us
  matrix products: 171 us -> 1.47 us
  other arithmetic: 107 us -> 6.19 us
  waiting for transfers between devices: 146 us -> 78.1 us
  Pallas kernels: 0 us -> 61.3 us
  between operations: 14.7 us -> 0.38 us
  starting transfers between devices: 16.4 us -> 27.4 us
    dot_general x113 -> x1, matrix products: 129 us -> 1.47 us  [per_device(): lax.dot_general(w_bias, normed_mid, (((0,), (2,)), ((), ())), preferred_e...]
    dynamic_slice x115 -> x1, local copies, waits for them, and re-layouts: 96.5 us -> 0.07 us  [per_device(): row_mask = lax.dynamic_slice_in_dim(key_mask, band_index * rows, rows)]
    unnamed x2 -> x0, waiting for transfers between devices: 76.3 us -> none
    pallas_call x0 -> x6, Pallas kernels: none -> 61.3 us  [the longest x1 37.6 us: per_device(): pl.pallas_call(functools.partial(attention_kernel, heads), grid=(rows,),...]
    div x16 -> x0, matrix products: 41.8 us -> none  [attend_row(): probs = exp_scores / jnp.sum(exp_scores, axis=-1, keepdims=True)]
    convert_element_type x22 -> x1, other arithmetic: 38 us -> 0.01 us  [per_device(): key_mask = residue_mask.astype(F32)]
    another operation x18 -> x0, other arithmetic: 34.8 us -> none
    unnamed x75 -> x47, local copies, waits for them, and re-layouts: 44.3 us -> 10.2 us
  transfers between devices with their start and end apart: 8 -> 5, of which waited for: 4 -> 5; matrix products, arithmetic and copies ran while one was open for 18% -> 3% of each run, Pallas kernels for 0% -> 6%
where the time goes in v1:
time: 251 us; the launch traced here: 248 us
  waiting for transfers between devices  78.1 us (31%)
  Pallas kernels  61.3 us (24%)
  blocking collectives  56.5 us (23%)
  starting transfers between devices  27.4 us (11%)
  local copies, waits for them, and re-layouts  17.2 us (7%)
  other arithmetic  6.19 us (2%)
    all_to_all x2, waiting for transfers between devices, collect(): back = lax.all_to_all(planes, AXES, split_axis=0, concat_axis=0, tiled=True)  42.7 us
    pallas_call x1, Pallas kernels, per_device(): pl.pallas_call(functools.partial(attention_kernel, heads), grid=(rows,),...  37.6 us
    all_to_all x1, blocking collectives, spread(): lax.all_to_all(planes, AXES, split_axis=0, concat_axis=0, tiled=True)  31.8 us
    all_to_all x2, waiting for transfers between devices, spread(): lax.all_to_all(planes, AXES, split_axis=0, concat_axis=0, tiled=True)  28 us
    all_gather x1, blocking collectives, per_device(): bias_full = lax.all_gather(bias_local, AXES, axis=1, tiled=True)  24.7 us
    all_to_all x2, starting transfers between devices, collect(): back = lax.all_to_all(planes, AXES, split_axis=0, concat_axis=0, tiled=True)  13.7 us
    pallas_call x2, Pallas kernels, run(): pl.pallas_call(kernel, grid=(rows // block,), in_specs=specs, out_specs=o...  11.3 us
    pallas_call x1, Pallas kernels, per_device(): pl.pallas_call(functools.partial(middle_kernel, split, heads), grid=(rows...  11.1 us
  transfers between devices with their start and end apart: 5, of which 5 were waited for; matrix products, arithmetic and copies ran while one was open for 3% of the time, Pallas kernels for 6%

profile of v1, /device:TPU:0, one launch (start us, length us, event | category | flops | bytes accessed | tf_op | source)
XLA Modules:
  0.0 248.4 jit_solution(940128137741983709)
XLA Ops:
  0.9 1.0 copy.25
  2.8 1.6 convert_reduce_fusion
  4.4 1.3 fusion.2
  5.7 1.5 fusion.5
  7.2 24.7 %all_gather.3 = bf16[4,256,256]{2,0,1:T(4,128)(2,1)S(1)} all-gather(bf16[4,16,256]{2,0,1:T(4,128)(2,1)S(1)} %fusion.5), channel_id=1, replica_groups=mesh['crop'=2,'ia'=8,'ja'=2] {'ia','ja'}, dimensions={1}, use_global_device_ids=true | all-gather | bytes 557056 | tf_op jit(solution)/shard_map/all_gather | solution.py:316
  31.9 1.1 copy.26
  33.0 1.2 add_bitcast_fusion.bias_ref
  34.3 37.6 %shard_map.145 = (f32[16,256,128]{2,1,0:T(8,128)S(1)}, bf16[4,256,256]{2,1,0:T(8,128)(2,1)S(1)}) custom-call(bf16[16,256,128]{2,1,0:T(8,128)(2,1)S(1)} %copy-done.1, bf16[16,256,128]{2,1,0:T(8,128)(2,1)S(1)} %copy-done.5, f32[1,128]{1,0:T(1,128)S(1)} %bitcast.48, bf16[512,128]{1,0:T(8,128)(2,1)S(1)} %bitcast.42, bf16[128,256]{1,0:T(8,128)(2,1)S(1)} %slice.12.wkv_ref, ...), custom_call_target="tpu_custom_call" | custom-call | flops 6442450944 | bytes 4194304 | tf_op jit(solution)/shard_map/pallas_call | solution.py:376
  71.8 1.3 copy-done.4
  74.0 4.2 %all-to-all-start = ((bf16[16,4,16,256]{3,2,1,0:T(8,128)(2,1)}), bf16[16,4,16,256]{3,2,1,0:T(8,128)(2,1)}, u32[]{:S(2)}, u32[]{:S(2)}) async-start(bf16[16,4,16,256]{3,2,1,0:T(8,128)(2,1)} %bitcast.51), calls=%async_computation | async-start | bytes 1048576 | tf_op jit(solution)/shard_map/all_to_all | solution.py:402
  80.9 3.6 %shard_map.147 = (bf16[16,16,8,256]{3,2,1,0:T(8,128)(2,1)S(1)}, bf16[16,16,8,256]{3,2,1,0:T(8,128)(2,1)}) custom-call(bf16[16,256,128]{2,1,0:T(8,128)(2,1)S(1)} %copy-done, f32[16,1,256]{2,1,0:T(1,128)S(1)} %broadcast_multiply_fusion.cell_ref, f32[1,128]{1,0:T(1,128)S(1)} %bitcast.45, bf16[512,128]{1,0:T(8,128)(2,1)S(1)} %pad_maximum_fusion.wt_ref), custom_call_target="tpu_custom_call" | custom-call | tf_op jit(solution)/shard_map/pallas_call | solution.py:347
  84.4 1.0 copy-done.8
  85.4 7.3 %all-to-all-done = bf16[16,4,16,256]{3,2,1,0:T(8,128)(2,1)} async-done(((bf16[16,4,16,256]{3,2,1,0:T(8,128)(2,1)}), bf16[16,4,16,256]{3,2,1,0:T(8,128)(2,1)}, u32[]{:S(2)}, u32[]{:S(2)}) %all-to-all-start) | async-done | bytes 524320 | tf_op jit(solution)/shard_map/all_to_all | solution.py:402
  92.7 4.4 %all-to-all-start.4 = ((bf16[16,16,8,256]{3,2,1,0:T(8,128)(2,1)}), bf16[16,16,8,256]{3,2,1,0:T(8,128)(2,1)}, u32[]{:S(2)}, u32[]{:S(2)}) async-start(bf16[16,16,8,256]{3,2,1,0:T(8,128)(2,1)} %copy-done.8), calls=%async_computation.4 | async-start | bytes 2097152 | tf_op jit(solution)/shard_map/all_to_all | solution.py:330
  97.2 1.1 convert_reduce_fusion.1
  98.4 11.1 %shard_map.146 = (f32[16,256,128]{2,1,0:T(8,128)}, bf16[16,256,128]{2,1,0:T(8,128)(2,1)S(1)}, bf16[16,16,8,256]{3,2,1,0:T(8,128)(2,1)S(1)}) custom-call(f32[16,256,128]{2,1,0:T(8,128)} %copy-done.4, f32[16,8,256]{2,1,0:T(8,128)S(1)} %pad.10.band_ref, f32[8,128]{1,0:T(8,128)S(1)} %pad_convert_fusion.wb_ref, bf16[16,256,128]{2,1,0:T(8,128)(2,1)S(1)} %copy-done.1, ...), custom_call_target="tpu_custom_call" | custom-call | tf_op jit(solution)/shard_map/pallas_call | solution.py:409
  109.5 1.0 copy-done.6
  110.5 1.0 copy-done.9
  111.5 8.5 %all-to-all-done.4 = bf16[16,16,8,256]{3,2,1,0:T(8,128)(2,1)} async-done(((bf16[16,16,8,256]{3,2,1,0:T(8,128)(2,1)}), bf16[16,16,8,256]{3,2,1,0:T(8,128)(2,1)}, u32[]{:S(2)}, u32[]{:S(2)}) %all-to-all-start.4) | async-done | bytes 1048608 | tf_op jit(solution)/shard_map/all_to_all | solution.py:330
  120.0 31.8 %all_to_all.30 = bf16[16,16,8,256]{3,2,1,0:T(8,128)(2,1)} all-to-all(bf16[16,16,8,256]{3,2,1,0:T(8,128)(2,1)} %copy-done.9), channel_id=1, replica_groups=mesh['crop'=2,'ia'=8,'ja'=2] {'ia','ja'}, dimensions={0} | all-to-all | bytes 2097152 | tf_op jit(solution)/shard_map/all_to_all | solution.py:330
  151.8 5.0 %all-to-all-start.2 = ((bf16[16,16,8,256]{3,2,1,0:T(8,128)(2,1)}), bf16[16,16,8,256]{3,2,1,0:T(8,128)(2,1)}, u32[]{:S(2)}, u32[]{:S(2)}) async-start(bf16[16,16,8,256]{3,2,1,0:T(8,128)(2,1)} %get-tuple-element.15), calls=%async_computation.2 | async-start | bytes 2097152 | tf_op jit(solution)/shard_map/all_to_all | solution.py:330
  156.8 1.5 copy.35
  159.3 1.0 copy-done.2
  160.3 19.5 %all-to-all-done.2 = bf16[16,16,8,256]{3,2,1,0:T(8,128)(2,1)} async-done(((bf16[16,16,8,256]{3,2,1,0:T(8,128)(2,1)}), bf16[16,16,8,256]{3,2,1,0:T(8,128)(2,1)}, u32[]{:S(2)}, u32[]{:S(2)}) %all-to-all-start.2) | async-done | bytes 1048608 | tf_op jit(solution)/shard_map/all_to_all | solution.py:330
  179.8 6.9 %all-to-all-start.5 = ((bf16[16,16,8,256]{3,2,1,0:T(8,128)(2,1)}), bf16[16,16,8,256]{3,2,1,0:T(8,128)(2,1)S(1)}, u32[]{:S(2)}, u32[]{:S(2)}) async-start(bf16[16,16,8,256]{3,2,1,0:T(8,128)(2,1)} %bitcast.36), calls=%async_computation.5 | async-start | bytes 2097152 | tf_op jit(solution)/shard_map/all_to_all | solution.py:337
  186.7 1.4 copy.34
  188.8 1.0 copy-done.3
  189.8 19.9 %all-to-all-done.5.right_ref = bf16[16,16,8,256]{3,2,1,0:T(8,128)(2,1)S(1)} async-done(((bf16[16,16,8,256]{3,2,1,0:T(8,128)(2,1)}), bf16[16,16,8,256]{3,2,1,0:T(8,128)(2,1)S(1)}, u32[]{:S(2)}, u32[]{:S(2)}) %all-to-all-start.5) | async-done | bytes 1048608 | tf_op jit(solution)/shard_map/all_to_all | solution.py:337
  209.6 6.9 %all-to-all-start.3 = ((bf16[16,16,8,256]{3,2,1,0:T(8,128)(2,1)}), bf16[16,16,8,256]{3,2,1,0:T(8,128)(2,1)S(1)}, u32[]{:S(2)}, u32[]{:S(2)}) async-start(bf16[16,16,8,256]{3,2,1,0:T(8,128)(2,1)} %bitcast.37), calls=%async_computation.3 | async-start | bytes 2097152 | tf_op jit(solution)/shard_map/all_to_all | solution.py:337
  216.6 22.8 %all-to-all-done.3.left_ref = bf16[16,16,8,256]{3,2,1,0:T(8,128)(2,1)S(1)} async-done(((bf16[16,16,8,256]{3,2,1,0:T(8,128)(2,1)}), bf16[16,16,8,256]{3,2,1,0:T(8,128)(2,1)S(1)}, u32[]{:S(2)}, u32[]{:S(2)}) %all-to-all-start.3) | async-done | bytes 1048608 | tf_op jit(solution)/shard_map/all_to_all | solution.py:337
  239.5 1.2 copy-done.7
  240.7 7.7 %shard_map.150 = f32[16,256,128]{2,1,0:T(8,128)} custom-call(bf16[16,16,8,256]{3,2,1,0:T(8,128)(2,1)S(1)} %all-to-all-done.3.left_ref, bf16[16,16,8,256]{3,2,1,0:T(8,128)(2,1)S(1)} %all-to-all-done.5.right_ref, bf16[16,256,128]{2,1,0:T(8,128)(2,1)S(1)} %copy-done.7, f32[16,256,128]{2,1,0:T(8,128)} %get-tuple-element.18.mid_ref, ...), custom_call_target="tpu_custom_call" | custom-call | tf_op jit(solution)/shard_map/pallas_call | solution.py:347
  (57 shorter events, 7.0 us)
Async XLA Ops:
  0.0 4.3 %copy-start.1 = (bf16[16,256,128]{2,1,0:T(8,128)(2,1)S(1)}, bf16[16,256,128]{2,1,0:T(8,128)(2,1)}, u32[]{:S(2)}) copy-start(bf16[16,256,128]{2,1,0:T(8,128)(2,1)} %mid_ref.3) | copy-start | bytes 3145732
  0.0 5.7 %copy-start.15 = (f32[128]{0:T(128)S(1)}, f32[128]{0:T(128)}, u32[]{:S(2)}) copy-start(f32[128]{0:T(128)} %param.26) | copy-start | bytes 1540
  0.0 5.7 %copy-start.20 = (bf16[128,4]{0,1:T(4,128)(2,1)S(1)}, bf16[128,4]{0,1:T(4,128)(2,1)}, u32[]{:S(2)}) copy-start(bf16[128,4]{0,1:T(4,128)(2,1)} %param.28) | copy-start | bytes 3076
  5.7 27.4 %copy-start.19 = (s32[256]{0:T(256)S(1)}, s32[256]{0:T(256)}, u32[]{:S(2)}) copy-start(s32[256]{0:T(256)} %param.19) | copy-start | bytes 3076
  7.2 27.1 %copy-start.5 = (bf16[16,256,128]{2,1,0:T(8,128)(2,1)S(1)}, bf16[16,256,128]{2,1,0:T(8,128)(2,1)}, u32[]{:S(2)}) copy-start(bf16[16,256,128]{2,1,0:T(8,128)(2,1)} %grad_ref.3) | copy-start | bytes 3145732
  7.2 27.1 %copy-start.17 = (bf16[128,128]{1,0:T(8,128)(2,1)S(1)}, bf16[128,128]{1,0:T(8,128)(2,1)}, u32[]{:S(2)}) copy-start(bf16[128,128]{1,0:T(8,128)(2,1)} %waout_ref.1) | copy-start | bytes 98308
  71.8 1.3 copy-start.4
  73.2 5.1 %copy-start.11 = (bf16[128,256]{1,0:T(8,128)(2,1)S(1)}, bf16[128,256]{1,0:T(8,128)(2,1)}, u32[]{:S(2)}) copy-start(bf16[128,256]{1,0:T(8,128)(2,1)} %wleft_ref.1) | copy-start | bytes 196612
  73.2 5.9 %copy-start.10 = (bf16[128,256]{1,0:T(8,128)(2,1)S(1)}, bf16[128,256]{1,0:T(8,128)(2,1)}, u32[]{:S(2)}) copy-start(bf16[128,256]{1,0:T(8,128)(2,1)} %wright_ref.1) | copy-start | bytes 196612
  73.2 7.7 %copy-start = (bf16[16,256,128]{2,1,0:T(8,128)(2,1)S(1)}, bf16[16,256,128]{2,1,0:T(8,128)(2,1)}, u32[]{:S(2)}) copy-start(bf16[16,256,128]{2,1,0:T(8,128)(2,1)} %pin_ref.5) | copy-start | bytes 3145732
  73.2 7.7 %copy-start.14 = (f32[128]{0:T(128)S(1)}, f32[128]{0:T(128)}, u32[]{:S(2)}) copy-start(f32[128]{0:T(128)} %param.20) | copy-start | bytes 1540
  74.0 18.7 %all-to-all-start = ((bf16[16,4,16,256]{3,2,1,0:T(8,128)(2,1)}), bf16[16,4,16,256]{3,2,1,0:T(8,128)(2,1)}, u32[]{:S(2)}, u32[]{:S(2)}) async-start(bf16[16,4,16,256]{3,2,1,0:T(8,128)(2,1)} %bitcast.51), calls=%async_computation | async-start | bytes 1048576 | tf_op jit(solution)/shard_map/all_to_all | solution.py:402
  78.3 18.8 %copy-start.12 = (bf16[128,128]{1,0:T(8,128)(2,1)S(1)}, bf16[128,128]{1,0:T(8,128)(2,1)}, u32[]{:S(2)}) copy-start(bf16[128,128]{1,0:T(8,128)(2,1)} %wtout_ref.1) | copy-start | bytes 98308
  80.8 17.6 %copy-start.13 = (bf16[128,128]{1,0:T(8,128)(2,1)S(1)}, bf16[128,128]{1,0:T(8,128)(2,1)}, u32[]{:S(2)}) copy-start(bf16[128,128]{1,0:T(8,128)(2,1)} %wtgate_ref.1) | copy-start | bytes 98308
  80.8 17.6 %copy-start.16 = (f32[128]{0:T(128)S(1)}, f32[128]{0:T(128)}, u32[]{:S(2)}) copy-start(f32[128]{0:T(128)} %param.24) | copy-start | bytes 1540
  84.4 1.0 copy-start.8
  92.7 27.3 %all-to-all-start.4 = ((bf16[16,16,8,256]{3,2,1,0:T(8,128)(2,1)}), bf16[16,16,8,256]{3,2,1,0:T(8,128)(2,1)}, u32[]{:S(2)}, u32[]{:S(2)}) async-start(bf16[16,16,8,256]{3,2,1,0:T(8,128)(2,1)} %copy-done.8), calls=%async_computation.4 | async-start | bytes 2097152 | tf_op jit(solution)/shard_map/all_to_all | solution.py:330
  109.5 1.0 copy-start.6
  110.5 1.0 copy-start.9
  151.8 28.0 %all-to-all-start.2 = ((bf16[16,16,8,256]{3,2,1,0:T(8,128)(2,1)}), bf16[16,16,8,256]{3,2,1,0:T(8,128)(2,1)}, u32[]{:S(2)}, u32[]{:S(2)}) async-start(bf16[16,16,8,256]{3,2,1,0:T(8,128)(2,1)} %get-tuple-element.15), calls=%async_computation.2 | async-start | bytes 2097152 | tf_op jit(solution)/shard_map/all_to_all | solution.py:330
  156.8 1.5 copy-start.18
  159.3 1.0 copy-start.2
  179.8 29.8 %all-to-all-start.5 = ((bf16[16,16,8,256]{3,2,1,0:T(8,128)(2,1)}), bf16[16,16,8,256]{3,2,1,0:T(8,128)(2,1)S(1)}, u32[]{:S(2)}, u32[]{:S(2)}) async-start(bf16[16,16,8,256]{3,2,1,0:T(8,128)(2,1)} %bitcast.36), calls=%async_computation.5 | async-start | bytes 2097152 | tf_op jit(solution)/shard_map/all_to_all | solution.py:337
  188.8 1.0 copy-start.3
  209.6 29.8 %all-to-all-start.3 = ((bf16[16,16,8,256]{3,2,1,0:T(8,128)(2,1)}), bf16[16,16,8,256]{3,2,1,0:T(8,128)(2,1)S(1)}, u32[]{:S(2)}, u32[]{:S(2)}) async-start(bf16[16,16,8,256]{3,2,1,0:T(8,128)(2,1)} %bitcast.37), calls=%async_computation.3 | async-start | bytes 2097152 | tf_op jit(solution)/shard_map/all_to_all | solution.py:337
  239.5 1.2 copy-start.7

commit v2 on v1

--- a/solution.py
+++ b/solution.py
@@ -75,36 +75,12 @@
         put_planes(right_ref, r, right, split)
 
 
-def attention_kernel(
-    heads,
-    mid_ref,
-    grad_ref,
-    gain_ref,
-    wt_ref,
-    wkv_ref,
-    wqg_ref,
-    wtkv_ref,
-    waout_ref,
-    bias_ref,
-    out_ref,
-    bias_out_ref,
-    q_block,
-    o_block,
-    acc,
+def attention_row(
+    heads, normed, grad_row, wt_ref, wkv_ref, wqg_ref, wtkv_ref, waout_ref, bias_ref, q_block, o_block, acc
 ):
-    step = pl.program_id(0)
-    length, channels = mid_ref.shape[1:]
+    length, channels = normed.shape
     dim = channels // heads
     scale = dim ** (-0.5)
-
-    @pl.when(step == 0)
-    def _():
-        q_block[...] = jnp.zeros_like(q_block)
-        o_block[...] = jnp.zeros_like(o_block)
-        acc[...] = jnp.zeros_like(acc)
-
-    unit, _ = standardize(mid_ref[0].astype(F32))
-    normed = (unit * gain_ref[...]).astype(BF16)
     proj = dot_t(wt_ref[...], normed)
     kv = dot(normed, wkv_ref[...]).astype(BF16)
     keys, values = kv[:, :channels], kv[:, channels:]
@@ -112,7 +88,7 @@
     values_t = proj[2 * channels : 3 * channels].astype(BF16)
     queries_t = proj[:channels].astype(BF16)
     gate = jax.nn.sigmoid(proj[3 * channels :])
-    gated = dot_t(waout_ref[...], grad_ref[0])
+    gated = dot_t(waout_ref[...], grad_row)
     out_t = (gated * gate).astype(BF16)
     for h in range(heads):
         rows = slice(h * dim, (h + 1) * dim)
@@ -141,12 +117,231 @@
     logit_grad = gated * attended * gate * (1.0 - gate)
     qg = jnp.concatenate([query_grad, logit_grad], axis=0).astype(BF16)
     kv_grad = jnp.concatenate([key_grad * scale, value_grad], axis=1).astype(BF16)
-    out_ref[0] = dot(kv_grad, wtkv_ref[...]) + dot(wqg_ref[...], qg).T
+    return dot(kv_grad, wtkv_ref[...]) + dot(wqg_ref[...], qg).T
+
+
+def attention_kernel(
+    heads,
+    mid_ref,
+    grad_ref,
+    gain_ref,
+    wt_ref,
+    wkv_ref,
+    wqg_ref,
+    wtkv_ref,
+    waout_ref,
+    bias_ref,
+    out_ref,
+    bias_out_ref,
+    q_block,
+    o_block,
+    acc,
+):
+    step = pl.program_id(0)
+
+    @pl.when(step == 0)
+    def _():
+        q_block[...] = jnp.zeros_like(q_block)
+        o_block[...] = jnp.zeros_like(o_block)
+        acc[...] = jnp.zeros_like(acc)
+
+    unit, _ = standardize(mid_ref[0].astype(F32))
+    normed = (unit * gain_ref[...]).astype(BF16)
+    out_ref[0] = attention_row(
+        heads, normed, grad_ref[0], wt_ref, wkv_ref, wqg_ref, wtkv_ref, waout_ref, bias_ref, q_block, o_block, acc
+    )
 
     @pl.when(step == pl.num_programs(0) - 1)
     def _():
         for h in range(heads):
             bias_out_ref[h] = acc[h].T.astype(BF16)
+
+
+def enter(me, count, second):
+    barrier = pltpu.get_barrier_semaphore()
+
+    def greet(p, carry):
+        other = lax.rem(me + p, count)
+        pl.semaphore_signal(
+            barrier, inc=1, device_id=place(other, second), device_id_type=pl.DeviceIdType.MESH
+        )
+        return carry
+
+    lax.fori_loop(1, count, greet, 0)
+    pl.semaphore_wait(barrier, count - 1)
+
+
+def place(index, second):
+    return {"ia": lax.div(index, second), "ja": lax.rem(index, second)}
+
+
+class Exchange:
+    def __init__(self, source, target, send, recv, slot, me, count, second, same=False):
+        self.source, self.target, self.same = source, target, same
+        self.send, self.recv, self.slot = send, recv, slot
+        self.me, self.count, self.second = me, count, second
+
+    def copy(self, p):
+        other = lax.rem(self.me + p, self.count)
+        return pltpu.make_async_remote_copy(
+            src_ref=self.source if self.same else self.source.at[other],
+            dst_ref=self.target.at[self.me],
+            send_sem=self.send.at[self.slot, p],
+            recv_sem=self.recv.at[self.slot, p],
+            device_id=place(other, self.second),
+            device_id_type=pl.DeviceIdType.MESH,
+        )
+
+    def start(self):
+        def go(p, carry):
+            self.copy(p).start()
+            return carry
+
+        lax.fori_loop(1, self.count, go, 0)
+        if self.same:
+            self.target[self.me] = self.source[...]
+        else:
+            self.target[self.me] = self.source[self.me]
+
+    def wait(self):
+        def go(p, carry):
+            self.copy(p).wait()
+            return carry
+
+        lax.fori_loop(1, self.count, go, 0)
+
+
+def position():
+    second = lax.axis_size("ja")
+    return (
+        lax.axis_index("ia") * second + lax.axis_index("ja"),
+        lax.axis_size("ia") * second,
+        second,
+    )
+
+
+def first_kernel(
+    heads,
+    in_ref,
+    mid_ref,
+    grad_ref,
+    cell_ref,
+    mask_ref,
+    tri_gain_ref,
+    att_gain_ref,
+    wt_edges_ref,
+    wb_ref,
+    wt_ref,
+    wkv_ref,
+    wqg_ref,
+    wtkv_ref,
+    waout_ref,
+    out_ref,
+    band_ref,
+    left_out_ref,
+    right_out_ref,
+    normed_ref,
+    bias_send,
+    bias_recv,
+    left_send,
+    left_recv,
+    right_send,
+    right_recv,
+    part_send,
+    part_recv,
+    bias_ref,
+    q_block,
+    o_block,
+    acc,
+    send,
+    recv,
+):
+    rows, length, channels = in_ref.shape
+    block = math.gcd(rows, 4)
+    me, count, second = position()
+    link = (send, recv)
+    bias_x = Exchange(bias_send, bias_recv, *link, 0, me, count, second, same=True)
+    left_x = Exchange(left_send, left_recv, *link, 1, me, count, second)
+    right_x = Exchange(right_send, right_recv, *link, 2, me, count, second)
+    part_x = Exchange(part_send, part_recv, *link, 3, me, count, second)
+
+    bias_rows = []
+    for b in range(rows // block):
+        part = slice(b * block, (b + 1) * block)
+        unit, _ = standardize(mid_ref[part].reshape(block * length, channels).astype(F32))
+        normed = (unit * att_gain_ref[...]).astype(BF16)
+        normed_ref[part] = normed.reshape(block, length, channels)
+        bias = dot_t(wb_ref[...], normed)
+        bias_rows += [bias[:, r * length : (r + 1) * length] for r in range(block)]
+    for h in range(heads):
+        bias_send[h] = jnp.concatenate([b[h : h + 1] for b in bias_rows], axis=0).astype(BF16)
+    enter(me, count, second)
+    bias_x.start()
+
+    def edges(b, carry):
+        part = pl.ds(b * block, block)
+        unit, _ = standardize(in_ref[part].reshape(block * length, channels).astype(F32))
+        proj = dot_t(wt_edges_ref[...], (unit * tri_gain_ref[...]).astype(BF16))
+        for r in range(block):
+            p = proj[:, r * length : (r + 1) * length]
+            cell = cell_ref[b * block + r]
+            left = cell * jax.nn.sigmoid(p[:channels]) * p[channels : 2 * channels]
+            right = cell * jax.nn.sigmoid(p[2 * channels : 3 * channels]) * p[3 * channels :]
+            shape = (count, channels // count, length)
+            left_send[:, b * block + r] = left.reshape(shape).astype(BF16)
+            right_send[:, b * block + r] = right.reshape(shape).astype(BF16)
+        return carry
+
+    lax.fori_loop(0, rows // block, edges, 0)
+    bias_x.wait()
+    left_x.start()
+    right_x.start()
+    q_block[...] = jnp.zeros_like(q_block)
+    o_block[...] = jnp.zeros_like(o_block)
+    acc[...] = jnp.zeros_like(acc)
+    for h in range(heads):
+        full = bias_recv[:, h].astype(F32).reshape(length, length)
+        bias_ref[h] = (full * math.log2(math.e) + mask_ref[...]).T
+
+    def attend(i, carry):
+        out_ref[i] = attention_row(
+            heads,
+            normed_ref[i],
+            grad_ref[i],
+            wt_ref,
+            wkv_ref,
+            wqg_ref,
+            wtkv_ref,
+            waout_ref,
+            bias_ref,
+            q_block,
+            o_block,
+            acc,
+        )
+        return carry
+
+    lax.fori_loop(0, rows, attend, 0)
+    for h in range(heads):
+        part_send[:, h] = acc[h].T.reshape(count, rows, length).astype(BF16)
+    part_x.start()
+    left_x.wait()
+    to_planes(left_recv, left_out_ref)
+    right_x.wait()
+    to_planes(right_recv, right_out_ref)
+    part_x.wait()
+    for h in range(heads):
+        band_ref[h] = jnp.sum(part_recv[:, h].astype(F32), axis=0)
+
+
+def to_planes(received, planes_ref):
+    count, rows = received.shape[:2]
+
+    def move(s, carry):
+        value = jnp.swapaxes(received[s].astype(F32), 0, 1).astype(BF16)
+        planes_ref[:, pl.ds(pl.multiple_of(s * rows, rows), rows), :] = value
+        return carry
+
+    lax.fori_loop(0, count, move, 0)
 
 
 def middle_kernel(
@@ -308,15 +503,6 @@
     w_qg = jnp.concatenate([w_qkvg[:, :channels], w_qkvg[:, 3 * channels :]], axis=1)
     wt_kv = wt_qkvg[channels : 3 * channels]
 
-    unit, _ = standardize(pair_mid.astype(F32))
-    normed_mid = (unit * att_gain).astype(BF16)
-    bias_local = lax.dot_general(
-        w_bias, normed_mid, (((0,), (2,)), ((), ())), preferred_element_type=F32
-    ).astype(BF16)
-    bias_full = lax.all_gather(bias_local, AXES, axis=1, tiled=True)
-    bias_t = jnp.swapaxes(bias_full, 1, 2).astype(F32) * math.log2(math.e)
-    bias_t = bias_t + jnp.where(residue_mask > 0, 0.0, -1e30)[None, :, None]
-
     if split:
         plane_shape = jax.ShapeDtypeStruct((devices, rows, group, length), BF16)
         plane_spec = pl.BlockSpec((devices, block, group, length), lambda i: (0, i, 0, 0))
@@ -353,54 +539,117 @@
             compiler_params=params(),
         )(*args)
 
-    left_act, right_act = run(
-        functools.partial(edge_kernel, split),
-        (pair_in, cell, tri_gain, wt_edges),
-        2,
-        (plane_shape, plane_shape),
-        (plane_spec, plane_spec),
-    )
-    left_planes, right_planes = spread(left_act), spread(right_act)
-
-    attention_args = (
-        pair_mid,
-        pair_grad,
-        att_gain,
-        wt_qkvg,
-        w_kv,
-        w_qg,
-        wt_kv,
-        w_aout,
-        bias_t,
-    )
-    normed_grad, bias_part = pl.pallas_call(
-        functools.partial(attention_kernel, heads),
-        grid=(rows,),
-        in_specs=[banded(a, 1) for a in attention_args[:2]]
-        + [whole(a) for a in attention_args[2:]],
-        out_specs=(
-            pl.BlockSpec((1, length, channels), lambda i: (i, 0, 0)),
-            pl.BlockSpec((heads, length, length), lambda i: (0, 0, 0)),
-        ),
-        out_shape=(
-            jax.ShapeDtypeStruct((rows, length, channels), F32),
-            jax.ShapeDtypeStruct((heads, length, length), BF16),
-        ),
-        scratch_shapes=[
-            pltpu.VMEM((heads, channels, length), BF16),
-            pltpu.VMEM((heads, channels, length), BF16),
-            pltpu.VMEM((heads, length, length), F32),
-        ],
-        compiler_params=params(),
-        cost_estimate=pl.CostEstimate(
-            flops=rows * heads * 12 * length * length * channels,
-            bytes_accessed=rows * length * channels * 8,
-            transcendentals=rows * heads * length * length,
-        ),
-    )(*attention_args)
-    bias_part = jnp.swapaxes(bias_part.reshape(heads, devices, rows, length), 0, 1)
-    bias_parts = lax.all_to_all(bias_part, AXES, split_axis=0, concat_axis=0, tiled=True)
-    band = jnp.swapaxes(jnp.sum(bias_parts.astype(F32), axis=0), 0, 1)
+    if split:
+        operands = (
+            pair_in,
+            pair_mid,
+            pair_grad,
+            cell,
+            jnp.where(residue_mask > 0, 0.0, -1e30)[None],
+            tri_gain,
+            att_gain,
+            wt_edges,
+            jnp.pad(w_bias.T, ((0, -heads % 16), (0, 0))),
+            wt_qkvg,
+            w_kv,
+            w_qg,
+            wt_kv,
+            w_aout,
+        )
+        vmem = pl.BlockSpec(memory_space=pltpu.VMEM)
+        planes = jax.ShapeDtypeStruct((group, length, length), BF16)
+        ones = pltpu.VMEM((devices, rows, group, length), BF16)
+        parts = pltpu.VMEM((devices, heads, rows, length), BF16)
+        normed_grad, band, left_planes, right_planes = pl.pallas_call(
+            functools.partial(first_kernel, heads),
+            in_specs=[vmem] * len(operands),
+            out_specs=[vmem] * 4,
+            out_shape=(
+                jax.ShapeDtypeStruct((rows, length, channels), F32),
+                jax.ShapeDtypeStruct((heads, rows, length), F32),
+                planes,
+                planes,
+            ),
+            scratch_shapes=[
+                pltpu.VMEM((rows, length, channels), BF16),
+                pltpu.VMEM((heads, rows, length), BF16),
+                parts,
+                ones,
+                ones,
+                ones,
+                ones,
+                parts,
+                parts,
+                pltpu.VMEM((heads, length, length), F32),
+                pltpu.VMEM((heads, channels, length), BF16),
+                pltpu.VMEM((heads, channels, length), BF16),
+                pltpu.VMEM((heads, length, length), F32),
+                pltpu.SemaphoreType.DMA((4, devices)),
+                pltpu.SemaphoreType.DMA((4, devices)),
+            ],
+            compiler_params=pltpu.CompilerParams(
+                collective_id=0, has_side_effects=True, vmem_limit_bytes=VMEM_BYTES
+            ),
+        )(*operands)
+        band = jnp.swapaxes(band, 0, 1)
+    else:
+        unit, _ = standardize(pair_mid.astype(F32))
+        normed_mid = (unit * att_gain).astype(BF16)
+        bias_local = lax.dot_general(
+            w_bias, normed_mid, (((0,), (2,)), ((), ())), preferred_element_type=F32
+        ).astype(BF16)
+        bias_full = lax.all_gather(bias_local, AXES, axis=1, tiled=True)
+        bias_t = jnp.swapaxes(bias_full, 1, 2).astype(F32) * math.log2(math.e)
+        bias_t = bias_t + jnp.where(residue_mask > 0, 0.0, -1e30)[None, :, None]
+
+        left_act, right_act = run(
+            functools.partial(edge_kernel, split),
+            (pair_in, cell, tri_gain, wt_edges),
+            2,
+            (plane_shape, plane_shape),
+            (plane_spec, plane_spec),
+        )
+        left_planes, right_planes = spread(left_act), spread(right_act)
+
+        attention_args = (
+            pair_mid,
+            pair_grad,
+            att_gain,
+            wt_qkvg,
+            w_kv,
+            w_qg,
+            wt_kv,
+            w_aout,
+            bias_t,
+        )
+        normed_grad, bias_part = pl.pallas_call(
+            functools.partial(attention_kernel, heads),
+            grid=(rows,),
+            in_specs=[banded(a, 1) for a in attention_args[:2]]
+            + [whole(a) for a in attention_args[2:]],
+            out_specs=(
+                pl.BlockSpec((1, length, channels), lambda i: (i, 0, 0)),
+                pl.BlockSpec((heads, length, length), lambda i: (0, 0, 0)),
+            ),
+            out_shape=(
+                jax.ShapeDtypeStruct((rows, length, channels), F32),
+                jax.ShapeDtypeStruct((heads, length, length), BF16),
+            ),
+            scratch_shapes=[
+                pltpu.VMEM((heads, channels, length), BF16),
+                pltpu.VMEM((heads, channels, length), BF16),
+                pltpu.VMEM((heads, length, length), F32),
+            ],
+            compiler_params=params(),
+            cost_estimate=pl.CostEstimate(
+                flops=rows * heads * 12 * length * length * channels,
+                bytes_accessed=rows * length * channels * 8,
+                transcendentals=rows * heads * length * length,
+            ),
+        )(*attention_args)
+        bias_part = jnp.swapaxes(bias_part.reshape(heads, devices, rows, length), 0, 1)
+        bias_parts = lax.all_to_all(bias_part, AXES, split_axis=0, concat_axis=0, tiled=True)
+        band = jnp.swapaxes(jnp.sum(bias_parts.astype(F32), axis=0), 0, 1)
     band = jnp.pad(band, ((0, 0), (0, -heads % 8), (0, 0)))
 
     row_spec = pl.BlockSpec((block, length, channels), lambda i: (i, 0, 0))

time: 251 us -> 210 us (0.84)
  waiting for transfers between devices: 78.1 us -> 42.9 us
  Pallas kernels: 61.3 us -> 95.9 us
  blocking collectives: 56.5 us -> 33.3 us
  starting transfers between devices: 27.4 us -> 11.9 us
  local copies, waits for them, and re-layouts: 17.2 us -> 20.1 us
  other arithmetic: 6.19 us -> 3.29 us
    pallas_call x1, Pallas kernels: 37.6 us -> 76 us  [per_device(): pl.pallas_call(functools.partial(first_kernel, heads), in_specs=[vmem] *...]
    all_to_all x3 -> x0, waiting for transfers between devices: 35.4 us -> none  [the longest x2 28 us: spread(): lax.all_to_all(planes, AXES, split_axis=0, concat_axis=0, tiled=True)]
    all_gather x1 -> x0, blocking collectives: 24.7 us -> none  [per_device(): bias_full = lax.all_gather(bias_local, AXES, axis=1, tiled=True)]
    all_to_all x3 -> x0, starting transfers between devices: 13.6 us -> none  [the longest x2 9.4 us: spread(): lax.all_to_all(planes, AXES, split_axis=0, concat_axis=0, tiled=True)]
    unnamed x47 -> x57, local copies, waits for them, and re-layouts: 10.2 us -> 17.4 us
    reduce_sum x3 -> x0, other arithmetic: 4 us -> none  [the longest x1 1.57 us: standardize(): average = jnp.mean(v, axis=-1, keepdims=True)]
    pallas_call x2 -> x1, Pallas kernels: 11.3 us -> 7.64 us  [run(): pl.pallas_call(kernel, grid=(rows // block,), in_specs=specs, out_specs=o...]
    all_to_all x3 -> x1, local copies, waits for them, and re-layouts: 3.16 us -> 0.21 us  [spread(): lax.all_to_all(planes, AXES, split_axis=0, concat_axis=0, tiled=True)]
  transfers between devices with their start and end apart: 5 -> 2, of which waited for: 5 -> 2; matrix products, arithmetic and copies ran while one was open for 3% -> 0% of each run, Pallas kernels for 6% -> 0%
where the time goes in v2:
time: 210 us; the launch traced here: 208 us
  Pallas kernels  95.9 us (46%)
  waiting for transfers between devices  42.9 us (20%)
  blocking collectives  33.3 us (16%)
  local copies, waits for them, and re-layouts  20.1 us (10%)
  starting transfers between devices  11.9 us (6%)
  other arithmetic  3.29 us (2%)
    pallas_call x1, Pallas kernels, per_device(): pl.pallas_call(functools.partial(first_kernel, heads), in_specs=[vmem] *...  76 us
    all_to_all x2, waiting for transfers between devices, collect(): back = lax.all_to_all(planes, AXES, split_axis=0, concat_axis=0, tiled=True)  42.9 us
    all_to_all x1, blocking collectives, spread(): lax.all_to_all(planes, AXES, split_axis=0, concat_axis=0, tiled=True)  33.3 us
    unnamed x57, local copies, waits for them, and re-layouts  17.4 us
    all_to_all x2, starting transfers between devices, collect(): back = lax.all_to_all(planes, AXES, split_axis=0, concat_axis=0, tiled=True)  11.9 us
    pallas_call x1, Pallas kernels, per_device(): pl.pallas_call(functools.partial(middle_kernel, split, heads), grid=(rows...  10.9 us
    pallas_call x1, Pallas kernels, run(): pl.pallas_call(kernel, grid=(rows // block,), in_specs=specs, out_specs=o...  7.64 us
  transfers between devices with their start and end apart: 2, of which 2 were waited for; matrix products, arithmetic and copies ran while one was open for 0% of the time, Pallas kernels for 0%

profile of v2, /device:TPU:0, one launch (start us, length us, event | category | flops | bytes accessed | tf_op | source)
XLA Modules:
  0.0 207.6 jit_solution(16895260672281695232)
XLA Ops:
  0.0 0.9 fusion
  0.9 1.0 copy.18
  1.9 0.8 slice.12.wkv_ref
  2.7 0.7 convert_element_type.10
  3.4 1.2 compare_select_fusion
  4.8 1.0 copy.16
  5.8 1.0 copy.17
  6.8 1.3 pad_convert_fusion.wb_ref
  8.0 0.7 pad.14.wb_ref
  8.8 1.2 copy-done.3
  10.0 1.2 copy-done.5
  11.2 0.8 copy-done.17
  12.0 0.7 copy-done.19
  12.6 0.7 copy-done.22
  13.3 0.7 copy-done.23
  14.0 76.0 %shard_map.145 = (f32[16,256,128]{2,1,0:T(8,128)}, f32[4,16,256]{2,1,0:T(8,128)S(1)}, bf16[8,256,256]{2,1,0:T(8,128)(2,1)S(1)}, bf16[8,256,256]{2,1,0:T(8,128)(2,1)S(1)}) custom-call(bf16[16,256,128]{2,1,0:T(8,128)(2,1)S(1)} %copy-done, bf16[16,256,128]{2,1,0:T(8,128)(2,1)S(1)} %copy-done.3, bf16[16,256,128]{2,1,0:T(8,128)(2,1)S(1)} %copy-done.5, ...), custom_call_target="tpu_custom_call" | custom-call | tf_op jit(solution)/shard_map/pallas_call | solution.py:563
  90.0 1.0 copy-done.9
  90.9 1.0 copy-done.11
  92.2 0.7 copy-done.18
  92.8 0.7 copy-done.20
  94.8 10.9 %shard_map.146 = (f32[16,256,128]{2,1,0:T(8,128)}, bf16[16,256,128]{2,1,0:T(8,128)(2,1)S(1)}, bf16[16,16,8,256]{3,2,1,0:T(8,128)(2,1)S(1)}) custom-call(f32[16,256,128]{2,1,0:T(8,128)} %get-tuple-element.12.ng_ref, f32[16,8,256]{2,1,0:T(8,128)S(1)} %pad.15.band_ref, f32[8,128]{1,0:T(8,128)S(1)} %copy-done.18, bf16[16,256,128]{2,1,0:T(8,128)(2,1)S(1)} %copy-done.4, ...), custom_call_target="tpu_custom_call" | custom-call | tf_op jit(solution)/shard_map/pallas_call | solution.py:658
  105.7 33.3 %all_to_all.15 = bf16[16,16,8,256]{3,2,1,0:T(8,128)(2,1)S(1)} all-to-all(bf16[16,16,8,256]{3,2,1,0:T(8,128)(2,1)S(1)} %get-tuple-element.14), channel_id=1, replica_groups=mesh['crop'=2,'ia'=8,'ja'=2] {'ia','ja'}, dimensions={0} | all-to-all | bytes 2097152 | tf_op jit(solution)/shard_map/all_to_all | solution.py:516
  139.3 0.7 shard_map.148
  140.0 1.0 copy-done.2
  141.0 5.0 %all-to-all-start.2 = ((bf16[16,16,8,256]{3,2,1,0:T(8,128)(2,1)}), bf16[16,16,8,256]{3,2,1,0:T(8,128)(2,1)S(1)}, u32[]{:S(2)}, u32[]{:S(2)}) async-start(bf16[16,16,8,256]{3,2,1,0:T(8,128)(2,1)} %bitcast.21), calls=%async_computation.2 | async-start | bytes 2097152 | tf_op jit(solution)/shard_map/all_to_all | solution.py:523
  146.0 1.2 copy-done.10
  147.9 1.0 copy-done.1
  148.8 20.1 %all-to-all-done.2.right_ref = bf16[16,16,8,256]{3,2,1,0:T(8,128)(2,1)S(1)} async-done(((bf16[16,16,8,256]{3,2,1,0:T(8,128)(2,1)}), bf16[16,16,8,256]{3,2,1,0:T(8,128)(2,1)S(1)}, u32[]{:S(2)}, u32[]{:S(2)}) %all-to-all-start.2) | async-done | bytes 1048608 | tf_op jit(solution)/shard_map/all_to_all | solution.py:523
  168.9 6.9 %all-to-all-start.1 = ((bf16[16,16,8,256]{3,2,1,0:T(8,128)(2,1)}), bf16[16,16,8,256]{3,2,1,0:T(8,128)(2,1)S(1)}, u32[]{:S(2)}, u32[]{:S(2)}) async-start(bf16[16,16,8,256]{3,2,1,0:T(8,128)(2,1)} %bitcast.20), calls=%async_computation.1 | async-start | bytes 2097152 | tf_op jit(solution)/shard_map/all_to_all | solution.py:523
  175.9 22.8 %all-to-all-done.1.left_ref = bf16[16,16,8,256]{3,2,1,0:T(8,128)(2,1)S(1)} async-done(((bf16[16,16,8,256]{3,2,1,0:T(8,128)(2,1)}), bf16[16,16,8,256]{3,2,1,0:T(8,128)(2,1)S(1)}, u32[]{:S(2)}, u32[]{:S(2)}) %all-to-all-start.1) | async-done | bytes 1048608 | tf_op jit(solution)/shard_map/all_to_all | solution.py:523
  198.8 1.2 copy-done.8
  200.0 7.6 %shard_map.149 = f32[16,256,128]{2,1,0:T(8,128)} custom-call(bf16[16,16,8,256]{3,2,1,0:T(8,128)(2,1)S(1)} %all-to-all-done.1.left_ref, bf16[16,16,8,256]{3,2,1,0:T(8,128)(2,1)S(1)} %all-to-all-done.2.right_ref, bf16[16,256,128]{2,1,0:T(8,128)(2,1)S(1)} %copy-done.8, f32[16,256,128]{2,1,0:T(8,128)} %get-tuple-element.18.mid_ref, ...), custom_call_target="tpu_custom_call" | custom-call | tf_op jit(solution)/shard_map/pallas_call | solution.py:533
  (49 shorter events, 2.7 us)
Async XLA Ops:
  0.0 8.8 %copy-start = (bf16[16,256,128]{2,1,0:T(8,128)(2,1)S(1)}, bf16[16,256,128]{2,1,0:T(8,128)(2,1)}, u32[]{:S(2)}) copy-start(bf16[16,256,128]{2,1,0:T(8,128)(2,1)} %pin_ref.3) | copy-start | bytes 3145732
  8.7 83.3 %copy-start.15 = (bf16[128,128]{1,0:T(8,128)(2,1)S(1)}, bf16[128,128]{1,0:T(8,128)(2,1)}, u32[]{:S(2)}) copy-start(bf16[128,128]{1,0:T(8,128)(2,1)} %wtout_ref.1) | copy-start | bytes 98308
  8.7 83.4 %copy-start.16 = (bf16[128,128]{1,0:T(8,128)(2,1)S(1)}, bf16[128,128]{1,0:T(8,128)(2,1)}, u32[]{:S(2)}) copy-start(bf16[128,128]{1,0:T(8,128)(2,1)} %wtgate_ref.1) | copy-start | bytes 98308
  8.8 1.2 copy-start.3
  10.0 1.2 copy-start.5
  11.2 0.8 copy-start.17
  12.0 0.7 copy-start.19
  12.6 0.7 copy-start.22
  13.3 0.7 copy-start.23
  14.0 78.2 %copy-start.4 = (bf16[16,256,128]{2,1,0:T(8,128)(2,1)S(1)}, bf16[16,256,128]{2,1,0:T(8,128)(2,1)}, u32[]{:S(2)}) copy-start(bf16[16,256,128]{2,1,0:T(8,128)(2,1)} %mid_ref.3) | copy-start | bytes 3145732
  14.0 78.2 %copy-start.6 = (bf16[16,256,128]{2,1,0:T(8,128)(2,1)S(1)}, bf16[16,256,128]{2,1,0:T(8,128)(2,1)}, u32[]{:S(2)}) copy-start(bf16[16,256,128]{2,1,0:T(8,128)(2,1)} %grad_ref.3) | copy-start | bytes 3145732
  89.9 1.0 copy-start.9
  90.9 1.0 copy-start.11
  92.2 0.7 copy-start.18
  92.8 0.7 copy-start.20
  93.5 0.7 copy-start.24
  94.1 0.7 copy-start.25
  105.7 33.5 %copy-start.7 = (bf16[16,256,128]{2,1,0:T(8,128)(2,1)}, bf16[16,256,128]{2,1,0:T(8,128)(2,1)S(1)}, u32[]{:S(2)}) copy-start(bf16[16,256,128]{2,1,0:T(8,128)(2,1)S(1)} %get-tuple-element.17.back_ref) | copy-start | bytes 3145732
  105.7 33.5 %copy-start.12 = (bf16[8,256,256]{2,1,0:T(8,128)(2,1)S(1)}, bf16[8,256,256]{2,1,0:T(8,128)(2,1)}, u32[]{:S(2)}) copy-start(bf16[8,256,256]{2,1,0:T(8,128)(2,1)} %copy-done.11) | copy-start | bytes 3145732
  140.0 1.0 copy-start.2
  141.0 27.9 %all-to-all-start.2 = ((bf16[16,16,8,256]{3,2,1,0:T(8,128)(2,1)}), bf16[16,16,8,256]{3,2,1,0:T(8,128)(2,1)S(1)}, u32[]{:S(2)}, u32[]{:S(2)}) async-start(bf16[16,16,8,256]{3,2,1,0:T(8,128)(2,1)} %bitcast.21), calls=%async_computation.2 | async-start | bytes 2097152 | tf_op jit(solution)/shard_map/all_to_all | solution.py:523
  146.0 1.2 copy-start.10
  147.2 51.5 %copy-start.13 = (bf16[128,256]{1,0:T(8,128)(2,1)S(1)}, bf16[128,256]{1,0:T(8,128)(2,1)}, u32[]{:S(2)}) copy-start(bf16[128,256]{1,0:T(8,128)(2,1)} %wright_ref.1) | copy-start | bytes 196612
  147.2 51.5 %copy-start.14 = (bf16[128,256]{1,0:T(8,128)(2,1)S(1)}, bf16[128,256]{1,0:T(8,128)(2,1)}, u32[]{:S(2)}) copy-start(bf16[128,256]{1,0:T(8,128)(2,1)} %wleft_ref.1) | copy-start | bytes 196612
  147.2 51.5 %copy-start.21 = (f32[128]{0:T(128)S(1)}, f32[128]{0:T(128)}, u32[]{:S(2)}) copy-start(f32[128]{0:T(128)} %param.20) | copy-start | bytes 1540
  147.9 1.0 copy-start.1
  168.9 29.8 %all-to-all-start.1 = ((bf16[16,16,8,256]{3,2,1,0:T(8,128)(2,1)}), bf16[16,16,8,256]{3,2,1,0:T(8,128)(2,1)S(1)}, u32[]{:S(2)}, u32[]{:S(2)}) async-start(bf16[16,16,8,256]{3,2,1,0:T(8,128)(2,1)} %bitcast.20), calls=%async_computation.1 | async-start | bytes 2097152 | tf_op jit(solution)/shard_map/all_to_all | solution.py:523
  198.7 1.2 copy-start.8

commit v3 on v2

--- a/solution.py
+++ b/solution.py
@@ -176,16 +176,20 @@
 
 
 class Exchange:
-    def __init__(self, source, target, send, recv, slot, me, count, second, same=False):
-        self.source, self.target, self.same = source, target, same
+    def __init__(self, source, target, send, recv, slot, me, count, second, same=False, part=None):
+        self.source, self.target, self.same, self.part = source, target, same, part
         self.send, self.recv, self.slot = send, recv, slot
         self.me, self.count, self.second = me, count, second
 
     def copy(self, p):
         other = lax.rem(self.me + p, self.count)
+        source = self.source if self.same else self.source.at[other]
+        target = self.target.at[self.me]
+        if self.part is not None:
+            source, target = source.at[self.part], target.at[self.part]
         return pltpu.make_async_remote_copy(
-            src_ref=self.source if self.same else self.source.at[other],
-            dst_ref=self.target.at[self.me],
+            src_ref=source,
+            dst_ref=target,
             send_sem=self.send.at[self.slot, p],
             recv_sem=self.recv.at[self.slot, p],
             device_id=place(other, self.second),
@@ -200,6 +204,8 @@
         lax.fori_loop(1, self.count, go, 0)
         if self.same:
             self.target[self.me] = self.source[...]
+        elif self.part is not None:
+            self.target[self.me, self.part] = self.source[self.me, self.part]
         else:
             self.target[self.me] = self.source[self.me]
 
@@ -389,6 +395,172 @@
     sum_grad = norm_grad(unit, rstd, sum_gain_ref[...], summed)
     for r in range(block):
         put_planes(planes_ref, r, sum_grad[r * length : (r + 1) * length].T, split)
+
+
+def second_kernel(
+    heads,
+    ng_ref,
+    band_ref,
+    wb_ref,
+    mid_ref,
+    grad_ref,
+    pin_ref,
+    sum_ref,
+    cell_ref,
+    left_ref,
+    right_ref,
+    att_gain_ref,
+    tri_gain_ref,
+    sum_gain_ref,
+    wtgate_ref,
+    wtgate_t_ref,
+    wtout_ref,
+    wtout_t_ref,
+    wt_edges_ref,
+    wleft_ref,
+    wright_ref,
+    out_ref,
+    mid_grad_ref,
+    back_ref,
+    coef_ref,
+    total_ref,
+    planes_ref,
+    grad_send,
+    grad_recv,
+    left_send,
+    left_recv,
+    right_send,
+    right_recv,
+    send,
+    recv,
+):
+    rows, length, channels = mid_ref.shape
+    block = math.gcd(rows, 4)
+    blocks = rows // block
+    me, count, second = position()
+
+    def grad_x(b):
+        part = pl.ds(b * block, block)
+        return Exchange(grad_send, grad_recv, send, recv, b, me, count, second, part=part)
+
+    def right_x(b):
+        part = pl.ds(b * block, block)
+        return Exchange(
+            right_send, right_recv, send, recv, blocks + b, me, count, second, part=part
+        )
+
+    left_x = Exchange(left_send, left_recv, send, recv, 2 * blocks, me, count, second)
+    enter(me, count, second)
+
+    def flat(ref, part):
+        return ref[part].reshape(block * length, channels)
+
+    def middle(b, carry):
+        part = pl.ds(b * block, block)
+        bias = []
+        for r in range(block):
+            band = band_ref[b * block + r].T
+            term = band[:, 0:1] * wb_ref[0:1]
+            for h in range(1, heads):
+                term = term + band[:, h : h + 1] * wb_ref[h : h + 1]
+            bias.append(term)
+        bias = jnp.concatenate(bias, axis=0)
+        unit, rstd = standardize(flat(mid_ref, part).astype(F32))
+        mid_grad = flat(grad_ref, part).astype(F32) + norm_grad(
+            unit, rstd, att_gain_ref[...], flat(ng_ref, part) + bias
+        )
+        unit, _ = standardize(flat(pin_ref, part).astype(F32))
+        gate = jax.nn.sigmoid(dot((unit * tri_gain_ref[...]).astype(BF16), wtgate_ref[...]))
+        unit, rstd = standardize(flat(sum_ref, part).astype(F32))
+        tri_out = dot((unit * sum_gain_ref[...]).astype(BF16), wtout_ref[...])
+        gated = mid_grad * gate
+        summed = dot(gated.astype(BF16), wtout_t_ref[...])
+        back = gated * tri_out * (1.0 - gate)
+        mid_grad_ref[part] = mid_grad.reshape(block, length, channels)
+        back_ref[part] = back.astype(BF16).reshape(block, length, channels)
+        sum_grad = norm_grad(unit, rstd, sum_gain_ref[...], summed)
+        for r in range(block):
+            value = sum_grad[r * length : (r + 1) * length].T
+            value = value.reshape(count, channels // count, length)
+            grad_send[:, b * block + r] = value.astype(BF16)
+        grad_x(b).start()
+        return carry
+
+    lax.fori_loop(0, blocks, middle, 0)
+
+    def prepare(b, carry):
+        part = pl.ds(b * block, block)
+        unit, _ = standardize(flat(pin_ref, part).astype(F32))
+        proj = dot_t(wt_edges_ref[...], (unit * tri_gain_ref[...]).astype(BF16))
+        for r in range(block):
+            cell = cell_ref[b * block + r]
+            for side in range(2):
+                p = proj[:, r * length : (r + 1) * length]
+                p = p[2 * side * channels : 2 * (side + 1) * channels]
+                s = jax.nn.sigmoid(p[:channels])
+                gate = cell * s
+                low = 2 * side * channels
+                coef_ref[b * block + r, low : low + channels] = gate * p[channels:] * (1.0 - s)
+                coef_ref[b * block + r, low + channels : low + 2 * channels] = gate
+        return carry
+
+    lax.fori_loop(0, blocks, prepare, 0)
+
+    def take(b, carry):
+        grad_x(b).wait()
+        return carry
+
+    lax.fori_loop(0, blocks, take, 0)
+    to_planes(grad_recv, planes_ref)
+    planes = planes_ref.shape[0]
+    outs = [dot(planes_ref[c], right_ref[c]) for c in range(planes)]
+    outs = jnp.swapaxes(jnp.stack(outs, axis=0), 0, 1)
+    left_send[...] = outs.reshape(left_send.shape).astype(BF16)
+    left_x.start()
+    outs = [dot(planes_ref[c].astype(F32).T.astype(BF16), left_ref[c]) for c in range(planes)]
+    outs = jnp.swapaxes(jnp.stack(outs, axis=0), 0, 1)
+    right_send[...] = outs.reshape(right_send.shape).astype(BF16)
+
+    def give(b, carry):
+        right_x(b).start()
+        return carry
+
+    lax.fori_loop(0, blocks, give, 0)
+
+    def edge_grad(received, w_ref, r, side):
+        grad = received[:, r].astype(F32).reshape(channels, length)
+        low = 2 * side * channels
+        first = grad * coef_ref[r, low : low + channels]
+        second_half = grad * coef_ref[r, low + channels : low + 2 * channels]
+        both = jnp.concatenate([first, second_half], axis=0).astype(BF16)
+        return dot(w_ref[...], both).T
+
+    left_x.wait()
+
+    def left_part(b, carry):
+        part = pl.ds(b * block, block)
+        gates = dot(flat(back_ref, part), wtgate_t_ref[...])
+        for r in range(block):
+            grad = edge_grad(left_recv, wleft_ref, b * block + r, 0)
+            total_ref[b * block + r] = gates[r * length : (r + 1) * length] + grad
+        return carry
+
+    lax.fori_loop(0, blocks, left_part, 0)
+
+    def finish(b, carry):
+        right_x(b).wait()
+        part = pl.ds(b * block, block)
+        grads = [
+            total_ref[b * block + r] + edge_grad(right_recv, wright_ref, b * block + r, 1)
+            for r in range(block)
+        ]
+        unit, rstd = standardize(flat(pin_ref, part).astype(F32))
+        total = jnp.concatenate(grads, axis=0)
+        result = flat(mid_grad_ref, part) + norm_grad(unit, rstd, tri_gain_ref[...], total)
+        out_ref[part] = result.reshape(block, length, channels)
+        return carry
+
+    lax.fori_loop(0, blocks, finish, 0)
 
 
 def left_kernel(grad_ref, right_ref, out_ref):
@@ -655,6 +827,53 @@
     row_spec = pl.BlockSpec((block, length, channels), lambda i: (i, 0, 0))
     row_shape = jax.ShapeDtypeStruct((rows, length, channels), F32)
     wb_t = jnp.pad(w_bias.astype(F32).T, ((0, -heads % 8), (0, 0)))
+    if split:
+        operands = (
+            normed_grad,
+            band,
+            wb_t,
+            pair_mid,
+            pair_grad,
+            pair_in,
+            tri_sum,
+            cell,
+            left_planes,
+            right_planes,
+            att_gain,
+            tri_gain,
+            sum_gain,
+            w_tgate,
+            w_tgate.T,
+            w_tout,
+            w_tout.T,
+            wt_edges,
+            w_left,
+            w_right,
+        )
+        return pl.pallas_call(
+            functools.partial(second_kernel, heads),
+            in_specs=[vmem] * len(operands),
+            out_specs=vmem,
+            out_shape=row_shape,
+            scratch_shapes=[
+                pltpu.VMEM((rows, length, channels), F32),
+                pltpu.VMEM((rows, length, channels), BF16),
+                pltpu.VMEM((rows, 4 * channels, length), F32),
+                pltpu.VMEM((rows, length, channels), F32),
+                pltpu.VMEM((group, length, length), BF16),
+                ones,
+                ones,
+                ones,
+                ones,
+                ones,
+                ones,
+                pltpu.SemaphoreType.DMA((2 * (rows // block) + 1, devices)),
+                pltpu.SemaphoreType.DMA((2 * (rows // block) + 1, devices)),
+            ],
+            compiler_params=pltpu.CompilerParams(
+                collective_id=1, has_side_effects=True, vmem_limit_bytes=VMEM_BYTES
+            ),
+        )(*operands)
     mid_grad, gate_back, sum_grad = pl.pallas_call(
         functools.partial(middle_kernel, split, heads),
         grid=(rows // block,),

time: 210 us -> 182 us (0.87)
  Pallas kernels: 95.9 us -> 163 us
  waiting for transfers between devices: 42.9 us -> 0 us
  blocking collectives: 33.3 us -> 0 us
  starting transfers between devices: 11.9 us -> 0 us
  local copies, waits for them, and re-layouts: 20.1 us -> 15.8 us
    pallas_call x4 -> x1, Pallas kernels: 19.9 us -> 87 us  [per_device(): pl.pallas_call(functools.partial(second_kernel, heads), in_specs=[vmem] *...]
    all_to_all x2 -> x0, waiting for transfers between devices: 42.9 us -> none  [collect(): back = lax.all_to_all(planes, AXES, split_axis=0, concat_axis=0, tiled=True)]
    all_to_all x1 -> x0, blocking collectives: 33.3 us -> none  [spread(): lax.all_to_all(planes, AXES, split_axis=0, concat_axis=0, tiled=True)]
    all_to_all x2 -> x0, starting transfers between devices: 11.9 us -> none  [collect(): back = lax.all_to_all(planes, AXES, split_axis=0, concat_axis=0, tiled=True)]
    unnamed x57 -> x32, local copies, waits for them, and re-layouts: 17.4 us -> 13.3 us
  transfers between devices with their start and end apart: 2 -> 0, of which waited for: 2 -> 0; matrix products, arithmetic and copies ran while one was open for 0% -> 0% of each run, Pallas kernels for 0% -> 0%
where the time goes in v3:
time: 182 us; the launch traced here: 181 us
  Pallas kernels  163 us (90%)
  local copies, waits for them, and re-layouts  15.8 us (9%)
  other arithmetic  2.23 us (1%)
    pallas_call x1, Pallas kernels, per_device(): pl.pallas_call(functools.partial(second_kernel, heads), in_specs=[vmem] *...  87 us
    pallas_call x1, Pallas kernels, per_device(): pl.pallas_call(functools.partial(first_kernel, heads), in_specs=[vmem] *...  76 us
    unnamed x32, local copies, waits for them, and re-layouts  13.3 us

profile of v3, /device:TPU:0, one launch (start us, length us, event | category | flops | bytes accessed | tf_op | source)
XLA Modules:
  0.0 181.1 jit_solution(17113809856380987039)
XLA Ops:
  0.0 0.8 convert_element_type.10
  0.8 0.1 dynamic_slice.3
  0.8 0.7 compare_select_fusion
  1.5 0.7 pad_convert_fusion.wb_ref
  2.2 0.7 pad.14.wb_ref
  2.9 0.1 broadcast_multiply_fusion.cell_ref
  3.0 0.9 copy.20
  3.9 0.9 copy.21
  4.7 1.0 copy.16
  5.7 1.0 copy.17
  6.7 0.8 slice.12.wkv_ref
  7.5 0.8 fusion
  8.3 0.0 copy-start.7
  8.3 0.0 copy-start.8
  8.3 1.0 copy.18
  9.4 0.0 copy-start.5
  9.4 0.0 copy-start.6
  9.4 0.0 copy-start.12
  9.4 0.0 copy-done
  9.4 0.0 copy-start.1
  9.4 1.2 copy-done.1
  10.7 1.2 copy-done.2
  11.9 0.8 copy-done.9
  12.7 0.7 copy-done.10
  13.3 0.7 copy-done.11
  14.0 76.0 %shard_map.145 = (f32[16,256,128]{2,1,0:T(8,128)}, f32[4,16,256]{2,1,0:T(8,128)S(1)}, bf16[8,256,256]{2,1,0:T(8,128)(2,1)S(1)}, bf16[8,256,256]{2,1,0:T(8,128)(2,1)S(1)}) custom-call(bf16[16,256,128]{2,1,0:T(8,128)(2,1)S(1)} %copy-done, bf16[16,256,128]{2,1,0:T(8,128)(2,1)S(1)} %copy-done.1, bf16[16,256,128]{2,1,0:T(8,128)(2,1)S(1)} %copy-done.2, ...), custom_call_target="tpu_custom_call" | custom-call | tf_op jit(solution)/shard_map/pallas_call | solution.py:735
  90.0 0.0 copy-start.4
  90.0 1.0 copy-done.4
  91.0 0.0 copy-done.7
  91.0 0.0 copy-done.8
  91.1 87.0 %shard_map.146 = f32[16,256,128]{2,1,0:T(8,128)} custom-call(f32[16,256,128]{2,1,0:T(8,128)} %get-tuple-element.9.ng_ref, f32[16,8,256]{2,1,0:T(8,128)S(1)} %pad.15.band_ref, f32[8,128]{1,0:T(8,128)S(1)} %pad_convert_fusion.wb_ref, bf16[16,256,128]{2,1,0:T(8,128)(2,1)S(1)} %copy-done.1, bf16[16,256,128]{2,1,0:T(8,128)(2,1)S(1)} %copy-done.2, ...), custom_call_target="tpu_custom_call" | custom-call | tf_op jit(solution)/shard_map/pallas_call | solution.py:853
  178.0 3.1 %copy.25 = f32[16,256,128]{2,1,0:T(8,128)} copy(f32[16,256,128]{2,1,0:T(8,128)} %shard_map.146) | data formatting | bytes 4194304
  (15 shorter events, 0.1 us)
Async XLA Ops:
  0.0 9.4 %copy-start = (bf16[16,256,128]{2,1,0:T(8,128)(2,1)S(1)}, bf16[16,256,128]{2,1,0:T(8,128)(2,1)}, u32[]{:S(2)}) copy-start(bf16[16,256,128]{2,1,0:T(8,128)(2,1)} %pin_ref.1) | copy-start | bytes 3145732
  8.3 82.7 %copy-start.7 = (bf16[128,128]{1,0:T(8,128)(2,1)S(1)}, bf16[128,128]{1,0:T(8,128)(2,1)}, u32[]{:S(2)}) copy-start(bf16[128,128]{1,0:T(8,128)(2,1)} %wtgate_ref.1) | copy-start | bytes 98308
  8.3 82.7 %copy-start.8 = (bf16[128,128]{1,0:T(8,128)(2,1)S(1)}, bf16[128,128]{1,0:T(8,128)(2,1)}, u32[]{:S(2)}) copy-start(bf16[128,128]{1,0:T(8,128)(2,1)} %wtout_ref.1) | copy-start | bytes 98308
  9.4 81.6 %copy-start.5 = (bf16[128,256]{1,0:T(8,128)(2,1)S(1)}, bf16[128,256]{1,0:T(8,128)(2,1)}, u32[]{:S(2)}) copy-start(bf16[128,256]{1,0:T(8,128)(2,1)} %wright_ref.1) | copy-start | bytes 196612
  9.4 81.6 %copy-start.6 = (bf16[128,256]{1,0:T(8,128)(2,1)S(1)}, bf16[128,256]{1,0:T(8,128)(2,1)}, u32[]{:S(2)}) copy-start(bf16[128,256]{1,0:T(8,128)(2,1)} %wleft_ref.1) | copy-start | bytes 196612
  9.4 81.6 %copy-start.12 = (f32[128]{0:T(128)S(1)}, f32[128]{0:T(128)}, u32[]{:S(2)}) copy-start(f32[128]{0:T(128)} %param.24) | copy-start | bytes 1540
  9.4 1.3 copy-start.1
  10.7 1.2 copy-start.2
  11.9 0.8 copy-start.9
  12.7 0.7 copy-start.10
  13.3 0.7 copy-start.11
  14.0 77.1 %copy-start.3 = (bf16[16,256,128]{2,1,0:T(8,128)(2,1)S(1)}, bf16[16,256,128]{2,1,0:T(8,128)(2,1)}, u32[]{:S(2)}) copy-start(bf16[16,256,128]{2,1,0:T(8,128)(2,1)} %sum_ref.1) | copy-start | bytes 3145732
  90.0 1.0 copy-start.4

commit v4 on v3

--- a/solution.py
+++ b/solution.py
@@ -235,12 +235,10 @@
     mask_ref,
     tri_gain_ref,
     att_gain_ref,
-    wt_edges_ref,
-    wb_ref,
-    wt_ref,
-    wkv_ref,
-    wqg_ref,
-    wtkv_ref,
+    w_left_ref,
+    w_right_ref,
+    w_bias_ref,
+    w_ref,
     waout_ref,
     out_ref,
     band_ref,
@@ -259,6 +257,12 @@
     q_block,
     o_block,
     acc,
+    wt_edges_ref,
+    wide_ref,
+    wt_ref,
+    wkv_ref,
+    wqg_ref,
+    wtkv_ref,
     send,
     recv,
 ):
@@ -271,18 +275,27 @@
     right_x = Exchange(right_send, right_recv, *link, 2, me, count, second)
     part_x = Exchange(part_send, part_recv, *link, 3, me, count, second)
 
+    wide_ref[...] = jnp.zeros_like(wide_ref)
+    wide_ref[:, :heads] = w_bias_ref[...].astype(F32)
+    w_bias_t = wide_ref[...].T[:16].astype(BF16)
     bias_rows = []
     for b in range(rows // block):
         part = slice(b * block, (b + 1) * block)
         unit, _ = standardize(mid_ref[part].reshape(block * length, channels).astype(F32))
         normed = (unit * att_gain_ref[...]).astype(BF16)
         normed_ref[part] = normed.reshape(block, length, channels)
-        bias = dot_t(wb_ref[...], normed)
+        bias = dot_t(w_bias_t, normed)
         bias_rows += [bias[:, r * length : (r + 1) * length] for r in range(block)]
     for h in range(heads):
         bias_send[h] = jnp.concatenate([b[h : h + 1] for b in bias_rows], axis=0).astype(BF16)
     enter(me, count, second)
     bias_x.start()
+    transposed_edges(w_left_ref, w_right_ref, wt_edges_ref)
+    wt_ref[...] = w_ref[...].astype(F32).T.astype(BF16)
+    wkv_ref[...] = w_ref[:, channels : 3 * channels]
+    wqg_ref[:, :channels] = w_ref[:, :channels]
+    wqg_ref[:, channels:] = w_ref[:, 3 * channels :]
+    wtkv_ref[...] = wt_ref[channels : 3 * channels]
 
     def edges(b, carry):
         part = pl.ds(b * block, block)
@@ -337,6 +350,12 @@
     part_x.wait()
     for h in range(heads):
         band_ref[h] = jnp.sum(part_recv[:, h].astype(F32), axis=0)
+
+
+def transposed_edges(w_left_ref, w_right_ref, out_ref):
+    half = w_left_ref.shape[1]
+    out_ref[:half] = w_left_ref[...].astype(F32).T.astype(BF16)
+    out_ref[half:] = w_right_ref[...].astype(F32).T.astype(BF16)
 
 
 def to_planes(received, planes_ref):
@@ -401,7 +420,7 @@
     heads,
     ng_ref,
     band_ref,
-    wb_ref,
+    w_bias_ref,
     mid_ref,
     grad_ref,
     pin_ref,
@@ -413,10 +432,7 @@
     tri_gain_ref,
     sum_gain_ref,
     wtgate_ref,
-    wtgate_t_ref,
     wtout_ref,
-    wtout_t_ref,
-    wt_edges_ref,
     wleft_ref,
     wright_ref,
     out_ref,
@@ -431,6 +447,9 @@
     left_recv,
     right_send,
     right_recv,
+    wt_edges_ref,
+    wide_ref,
+    wb_ref,
     send,
     recv,
 ):
@@ -450,6 +469,9 @@
         )
 
     left_x = Exchange(left_send, left_recv, send, recv, 2 * blocks, me, count, second)
+    wide_ref[...] = jnp.zeros_like(wide_ref)
+    wide_ref[:, :heads] = w_bias_ref[...].astype(F32)
+    wb_ref[...] = wide_ref[...].T
     enter(me, count, second)
 
     def flat(ref, part):
@@ -474,7 +496,7 @@
         unit, rstd = standardize(flat(sum_ref, part).astype(F32))
         tri_out = dot((unit * sum_gain_ref[...]).astype(BF16), wtout_ref[...])
         gated = mid_grad * gate
-        summed = dot(gated.astype(BF16), wtout_t_ref[...])
+        summed = dot_t(gated.astype(BF16), wtout_ref[...])
         back = gated * tri_out * (1.0 - gate)
         mid_grad_ref[part] = mid_grad.reshape(block, length, channels)
         back_ref[part] = back.astype(BF16).reshape(block, length, channels)
@@ -487,6 +509,7 @@
         return carry
 
     lax.fori_loop(0, blocks, middle, 0)
+    transposed_edges(wleft_ref, wright_ref, wt_edges_ref)
 
     def prepare(b, carry):
         part = pl.ds(b * block, block)
@@ -539,7 +562,7 @@
 
     def left_part(b, carry):
         part = pl.ds(b * block, block)
-        gates = dot(flat(back_ref, part), wtgate_t_ref[...])
+        gates = dot_t(flat(back_ref, part), wtgate_ref[...])
         for r in range(block):
             grad = edge_grad(left_recv, wleft_ref, b * block + r, 0)
             total_ref[b * block + r] = gates[r * length : (r + 1) * length] + grad
@@ -720,12 +743,10 @@
             jnp.where(residue_mask > 0, 0.0, -1e30)[None],
             tri_gain,
             att_gain,
-            wt_edges,
-            jnp.pad(w_bias.T, ((0, -heads % 16), (0, 0))),
-            wt_qkvg,
-            w_kv,
-            w_qg,
-            wt_kv,
+            w_left,
+            w_right,
+            w_bias,
+            w_qkvg,
             w_aout,
         )
         vmem = pl.BlockSpec(memory_space=pltpu.VMEM)
@@ -756,6 +777,12 @@
                 pltpu.VMEM((heads, channels, length), BF16),
                 pltpu.VMEM((heads, channels, length), BF16),
                 pltpu.VMEM((heads, length, length), F32),
+                pltpu.VMEM((4 * channels, channels), BF16),
+                pltpu.VMEM((channels, channels), F32),
+                pltpu.VMEM((4 * channels, channels), BF16),
+                pltpu.VMEM((channels, 2 * channels), BF16),
+                pltpu.VMEM((channels, 2 * channels), BF16),
+                pltpu.VMEM((2 * channels, channels), BF16),
                 pltpu.SemaphoreType.DMA((4, devices)),
                 pltpu.SemaphoreType.DMA((4, devices)),
             ],
@@ -831,7 +858,7 @@
         operands = (
             normed_grad,
             band,
-            wb_t,
+            w_bias,
             pair_mid,
             pair_grad,
             pair_in,
@@ -843,10 +870,7 @@
             tri_gain,
             sum_gain,
             w_tgate,
-            w_tgate.T,
             w_tout,
-            w_tout.T,
-            wt_edges,
             w_left,
             w_right,
         )
@@ -867,6 +891,9 @@
                 ones,
                 ones,
                 ones,
+                pltpu.VMEM((4 * channels, channels), BF16),
+                pltpu.VMEM((channels, channels), F32),
+                pltpu.VMEM((channels, channels), F32),
                 pltpu.SemaphoreType.DMA((2 * (rows // block) + 1, devices)),
                 pltpu.SemaphoreType.DMA((2 * (rows // block) + 1, devices)),
             ],

time: 182 us -> 179 us (0.984)
  local copies, waits for them, and re-layouts: 15.8 us -> 13.4 us
where the time goes in v4:
time: 179 us; the launch traced here: 178 us
  Pallas kernels  163 us (91%)
  local copies, waits for them, and re-layouts  13.4 us (7%)
    pallas_call x1, Pallas kernels, per_device(): pl.pallas_call(functools.partial(second_kernel, heads), in_specs=[vmem] *...  87.2 us
    pallas_call x1, Pallas kernels, per_device(): pl.pallas_call(functools.partial(first_kernel, heads), in_specs=[vmem] *...  76 us
    unnamed x32, local copies, waits for them, and re-layouts  13.2 us

profile of v4, /device:TPU:0, one launch (start us, length us, event | category | flops | bytes accessed | tf_op | source)
XLA Modules:
  0.0 178.2 jit_solution(14774270569464498725)
XLA Ops:
  0.0 0.0 copy-start.6
  0.0 0.0 copy-start.14
  0.0 0.7 convert_element_type.5
  0.7 0.1 dynamic_slice.3
  0.8 0.7 compare_select_fusion
  1.5 0.1 broadcast_multiply_fusion.cell_ref
  1.6 0.8 copy.16.w_bias_ref
  2.4 0.0 copy-start
  2.4 1.2 copy-done
  3.6 0.0 copy-start.1
  3.6 1.2 copy-done.1
  4.8 0.0 copy-start.2
  4.8 1.2 copy-done.2
  6.0 0.0 copy-start.5
  6.1 0.8 copy-done.5
  6.9 0.0 copy-start.7
  6.9 0.8 copy-done.7
  7.7 0.0 copy-start.8
  7.7 0.9 copy-done.8
  8.6 0.8 copy-done.9
  9.4 0.7 copy-done.12
  10.1 0.7 copy-done.13
  10.7 76.0 %shard_map.145 = (f32[16,256,128]{2,1,0:T(8,128)}, f32[4,16,256]{2,1,0:T(8,128)S(1)}, bf16[8,256,256]{2,1,0:T(8,128)(2,1)S(1)}, bf16[8,256,256]{2,1,0:T(8,128)(2,1)S(1)}) custom-call(bf16[16,256,128]{2,1,0:T(8,128)(2,1)S(1)} %copy-done, bf16[16,256,128]{2,1,0:T(8,128)(2,1)S(1)} %copy-done.1, bf16[16,256,128]{2,1,0:T(8,128)(2,1)S(1)} %copy-done.2, ...), custom_call_target="tpu_custom_call" | custom-call | tf_op jit(solution)/shard_map/pallas_call | solution.py:756
  86.7 0.0 copy-start.4
  86.7 1.0 copy-done.4
  87.8 0.0 copy-done.6
  87.8 0.0 copy-done.14
  87.8 0.0 copy-done.3
  87.8 0.0 copy-done.10
  87.8 0.0 copy-done.11
  87.8 87.2 %shard_map.146 = f32[16,256,128]{2,1,0:T(8,128)} custom-call(f32[16,256,128]{2,1,0:T(8,128)} %get-tuple-element.9.ng_ref, f32[16,8,256]{2,1,0:T(8,128)S(1)} %pad.4.band_ref, bf16[128,4]{1,0:T(8,128)(2,1)S(1)} %copy.16.w_bias_ref, bf16[16,256,128]{2,1,0:T(8,128)(2,1)S(1)} %copy-done.1, bf16[16,256,128]{2,1,0:T(8,128)(2,1)S(1)} %copy-done.2, ...), custom_call_target="tpu_custom_call" | custom-call | tf_op jit(solution)/shard_map/pallas_call | solution.py:877
  175.1 3.1 %copy.22 = f32[16,256,128]{2,1,0:T(8,128)} copy(f32[16,256,128]{2,1,0:T(8,128)} %shard_map.146) | data formatting | bytes 4194304
  (8 shorter events, 0.1 us)
Async XLA Ops:
  0.0 87.8 %copy-start.6 = (bf16[128,256]{1,0:T(8,128)(2,1)S(1)}, bf16[128,256]{1,0:T(8,128)(2,1)}, u32[]{:S(2)}) copy-start(bf16[128,256]{1,0:T(8,128)(2,1)} %wleft_ref.1) | copy-start | bytes 196612
  0.0 87.8 %copy-start.14 = (f32[128]{0:T(128)S(1)}, f32[128]{0:T(128)}, u32[]{:S(2)}) copy-start(f32[128]{0:T(128)} %param.24) | copy-start | bytes 1540
  2.4 1.2 copy-start
  3.6 1.2 copy-start.1
  4.8 1.2 copy-start.2
  6.0 0.8 copy-start.5
  6.9 0.8 copy-start.7
  7.7 0.9 copy-start.8
  8.6 0.8 copy-start.9
  9.4 0.7 copy-start.12
  10.0 0.7 copy-start.13
  10.7 77.1 %copy-start.3 = (bf16[16,256,128]{2,1,0:T(8,128)(2,1)S(1)}, bf16[16,256,128]{2,1,0:T(8,128)(2,1)}, u32[]{:S(2)}) copy-start(bf16[16,256,128]{2,1,0:T(8,128)(2,1)} %sum_ref.1) | copy-start | bytes 3145732
  10.7 77.1 %copy-start.10 = (bf16[128,128]{1,0:T(8,128)(2,1)S(1)}, bf16[128,128]{1,0:T(8,128)(2,1)}, u32[]{:S(2)}) copy-start(bf16[128,128]{1,0:T(8,128)(2,1)} %wtgate_ref.1) | copy-start | bytes 98308
  10.7 77.1 %copy-start.11 = (bf16[128,128]{1,0:T(8,128)(2,1)S(1)}, bf16[128,128]{1,0:T(8,128)(2,1)}, u32[]{:S(2)}) copy-start(bf16[128,128]{1,0:T(8,128)(2,1)} %wtout_ref.1) | copy-start | bytes 98308
  86.7 1.0 copy-start.4
